TPU v7x, 768 devices: a whole 4x8x12 slice. The times are simulated.
768 devices in a mesh: curve: 96 (over y, z), sub: 8 (over x, core).
Axes of the slice: x: 4, y: 8, z: 12, core: 2. Of those that a mesh axis runs over, the one named last changes fastest.
Arguments:
- state_now: float32 [5, 125, 98304], P(None, None, ('curve', 'sub')), may hold values from -0.5 to 4, as said below
- section_memory: float32 [5, 125, 98304], P(None, None, ('curve', 'sub')), may hold values from -3 to 3
- element_level: int32 [98304], P(('curve', 'sub')), may hold values from 0 to 1
- face_kind: int32 [6, 98304], P(None, ('curve', 'sub')), may hold values from 0 to 2
- face_partner: int32 [4, 6, 98304], P(None, None, ('curve', 'sub')), may hold values from 0 to 351
- face_quadrant: int32 [6, 98304], P(None, ('curve', 'sub')), may hold values from 0 to 3
- send_sub: int32 [6144, 3, 4], P(('curve', 'sub')), may hold values from 0 to 255
- send_curve: int32 [1536, 3, 32], P(('curve', 'sub')), may hold values from 0 to 255
Outputs:
- state_next: float32 [5, 125, 98304], P(None, None, ('curve', 'sub'))
- memory_next: float32 [5, 125, 98304], P(None, None, ('curve', 'sub'))
Inputs may be any that keep to these rules, and one draw needn't show every extreme that they name: `state_now`: density and pressure lie between 0.75 and 1.25 at every point and each velocity component is at most 0.35 in size; the last variable is pressure / 0.4 plus the kinetic energy. `face_partner`: values below 256 name this device's faces of the face's direction (side times 128 plus element); the next 32 the faces received from the sub peers (peer times 4 plus slot); the last 64 those from the previous and then the next curve device. Rows 1 to 3 are read only for faces of kind 2. `send_sub`: each entry names a face of this device of the given direction (side times 128 plus element). `send_curve`: row 0 of a device goes to the previous curve device, row 1 to the next; entries as in send_sub. `face_kind`: 0 conforming, 1 small side of a 2:1 mortar, 2 big side.
All inputs are finite; a program needn't handle non-finite values.
Results may differ from a plain program's by a relative error of at most 0.0003.
Values sent between devices are 32-bit elements; how exact they have to be, the bound alone decides.
No kernel may reach another device: no remote copies, remote signals or barrier semaphores. Data moves between devices by JAX's collectives and lax.ppermute only.
A program may use at most 128 MiB of HBM per device.

v0:
```python
import math

import jax
import jax.numpy as jnp
import numpy as np
from jax import lax
from jax.sharding import PartitionSpec as P

viscosity = 0.1
conduction = 0.1 * 1.4 / (0.4 * 0.72)
time_step = 0.02
section_decay = -567301805773.0 / 1357537059087.0
section_weight = 5161836677717.0 / 13612068292357.0
highest = lax.Precision.HIGHEST


def extended(cells, sides, width):
    for axis, dim in sides:
        count = lax.axis_size(axis)
        head = lax.slice_in_dim(cells, 0, width, axis=dim)
        tail = lax.slice_in_dim(cells, cells.shape[dim] - width, cells.shape[dim], axis=dim)
        cells = jnp.concatenate(
            [
                lax.ppermute(tail, axis, [(i, (i + 1) % count) for i in range(count)]),
                cells,
                lax.ppermute(head, axis, [((i + 1) % count, i) for i in range(count)]),
            ],
            axis=dim,
        )
    return cells


def derivative_numbers():
    gl_nodes = np.array([-1.0, -math.sqrt(3.0 / 7.0), 0.0, math.sqrt(3.0 / 7.0), 1.0])
    products = np.array(
        [np.prod([gl_nodes[m] - gl_nodes[k] for k in range(5) if k != m]) for m in range(5)]
    )
    derivative = np.zeros((5, 5))
    for i in range(5):
        for m in range(5):
            if i != m:
                derivative[i, m] = products[i] / products[m] / (gl_nodes[i] - gl_nodes[m])
        derivative[i, i] = -np.sum(derivative[i])
    return derivative


def gl_tables():
    gl_nodes = np.array([-1.0, -math.sqrt(3.0 / 7.0), 0.0, math.sqrt(3.0 / 7.0), 1.0])
    gl_weights = np.array([0.1, 49.0 / 90.0, 32.0 / 45.0, 49.0 / 90.0, 0.1])
    derivative = derivative_numbers()

    def lagrange(points):
        values = np.ones((5, 5))
        for m in range(5):
            for k in range(5):
                if k != m:
                    values[:, m] = (
                        values[:, m] * (points - gl_nodes[k]) / (gl_nodes[m] - gl_nodes[k])
                    )
        return values

    halves = [lagrange((gl_nodes - 1.0) / 2.0), lagrange((gl_nodes + 1.0) / 2.0)]
    projections = [
        0.5 * (half_map * gl_weights[:, None]).T / gl_weights[:, None] for half_map in halves
    ]
    interp_table = np.stack([np.kron(halves[a], halves[b]) for a in range(2) for b in range(2)])
    project_table = np.stack(
        [np.kron(projections[a], projections[b]) for a in range(2) for b in range(2)]
    )
    return (
        derivative,
        jnp.asarray(interp_table, dtype=jnp.float32),
        jnp.asarray(project_table, dtype=jnp.float32),
        float(gl_weights[0]),
    )


def primitives(conserved):
    density = conserved[0]
    velocity = conserved[1:4] / density
    pressure = 0.4 * (conserved[4] - 0.5 * jnp.sum(conserved[1:4] * velocity, axis=0))
    return (density, velocity, pressure)


def euler_flux(conserved, direction):
    density, velocity, pressure = primitives(conserved)
    normal_speed = velocity[direction]
    flux_rows = [conserved[1 + direction]]
    for k in range(3):
        flux_term = conserved[1 + k] * normal_speed
        if k == direction:
            flux_term = flux_term + pressure
        flux_rows.append(flux_term)
    flux_rows.append((conserved[4] + pressure) * normal_speed)
    return jnp.stack(flux_rows)


def signal_speed(conserved, direction):
    density, velocity, pressure = primitives(conserved)
    return jnp.abs(velocity[direction]) + jnp.sqrt(1.4 * pressure / density)


def face_flux(minus_side, plus_side, direction, normal_sign):
    fastest = jnp.maximum(signal_speed(minus_side, direction), signal_speed(plus_side, direction))
    return 0.5 * normal_sign * (
        euler_flux(minus_side, direction) + euler_flux(plus_side, direction)
    ) - 0.5 * fastest * (plus_side - minus_side)


def gradient_inputs(conserved):
    density, velocity, pressure = primitives(conserved)
    return jnp.concatenate([velocity, (pressure / density)[None]], axis=0)


def viscous_flux(conserved, gradients, direction):
    density, velocity, pressure = primitives(conserved)
    divergence = gradients[0] + gradients[4] + gradients[8]
    stresses = []
    for k in range(3):
        stress = viscosity * (gradients[3 * direction + k] + gradients[3 * k + direction])
        if k == direction:
            stress = stress - 2.0 / 3.0 * viscosity * divergence
        stresses.append(stress)
    heat_flux = velocity[0] * stresses[0] + velocity[1] * stresses[1] + velocity[2] * stresses[2]
    heat_flux = heat_flux + conduction * gradients[9 + direction]
    return jnp.stack(stresses + [heat_flux])


def line_slices(nodal_field, axis):
    return [lax.index_in_dim(nodal_field, m, axis, keepdims=False) for m in range(5)]


def along_axis(nodal_field, derivative, direction):
    pieces = line_slices(nodal_field, 3 - direction)
    outputs = []
    for i in range(5):
        total = float(derivative[i, 0]) * pieces[0]
        for m in range(1, 5):
            total = total + float(derivative[i, m]) * pieces[m]
        outputs.append(total)
    return jnp.stack(outputs, axis=3 - direction)


def split_volume(conserved, derivative, direction):
    density, velocity, pressure = primitives(conserved)
    enthalpy = (conserved[4] + pressure) / density
    axis = 2 - direction
    rho_s = line_slices(density, axis)
    normal_s = line_slices(velocity[direction], axis)
    vel_s = [line_slices(velocity[k], axis) for k in range(3)]
    press_s = line_slices(pressure, axis)
    enth_s = line_slices(enthalpy, axis)
    pairs = {}
    for i in range(5):
        for m in range(i, 5):
            mass_flux = 0.5 * (rho_s[i] + rho_s[m]) * (0.5 * (normal_s[i] + normal_s[m]))
            rows = [mass_flux]
            for pair_k in range(3):
                pair_term = mass_flux * (0.5 * (vel_s[pair_k][i] + vel_s[pair_k][m]))
                if pair_k == direction:
                    pair_term = pair_term + 0.5 * (press_s[i] + press_s[m])
                rows.append(pair_term)
            rows.append(mass_flux * (0.5 * (enth_s[i] + enth_s[m])))
            pairs[i, m] = jnp.stack(rows)
    outputs = []
    for i in range(5):
        total = None
        for m in range(5):
            term = float(2.0 * derivative[i, m]) * pairs[min(i, m), max(i, m)]
            total = term if total is None else total + term
        outputs.append(total)
    return jnp.stack(outputs, axis=3 - direction)


def face_trace(nodal_field, direction, s):
    picked = jnp.take(nodal_field, 4 * s, axis=3 - direction)
    return picked.reshape(picked.shape[0], 25, picked.shape[-1])


def axis_traces(nodal_field, direction):
    return jnp.concatenate(
        [face_trace(nodal_field, direction, 0), face_trace(nodal_field, direction, 1)], axis=-1
    )


def add_faces(nodal_field, direction, values):
    elements = nodal_field.shape[-1]
    for s in range(2):
        where_face = [slice(None)] * 5
        where_face[3 - direction] = 4 * s
        face_block = values[:, :, s * elements : (s + 1) * elements].reshape(
            values.shape[0], 5, 5, elements
        )
        nodal_field = nodal_field.at[tuple(where_face)].add(face_block)
    return nodal_field


def face_signs(elements):
    return jnp.where(jnp.arange(2 * elements) >= elements, 1.0, -1.0).astype(jnp.float32)


def axis_info(face_kind, face_partner, face_quadrant, direction):
    axis_kinds = face_kind[2 * direction : 2 * direction + 2].reshape(-1)
    axis_partners = face_partner[:, 2 * direction : 2 * direction + 2].reshape(4, -1)
    axis_quadrants = face_quadrant[2 * direction : 2 * direction + 2].reshape(-1)
    return (axis_kinds, axis_partners, axis_quadrants)


def spread_faces(interp_table, faces):
    moved = jnp.tensordot(interp_table, faces, axes=([2], [1]), precision=highest)
    return jnp.moveaxis(moved, 2, 1)


def project_faces(project_table, parts):
    total = None
    for q in range(4):
        term = jnp.tensordot(project_table[q], parts[q], axes=([1], [1]), precision=highest)
        total = term if total is None else total + term
    return jnp.moveaxis(total, 0, 1)


def mortar_states(pool, own_faces, axis_kinds, axis_partners, axis_quadrants, interp_table):
    first_partner = jnp.take(pool, axis_partners[0], axis=2)
    spread = spread_faces(interp_table, first_partner)
    chosen = axis_quadrants[None, None, None, :] == jnp.arange(4)[:, None, None, None]
    picked = jnp.sum(jnp.where(chosen, spread, 0.0), axis=0)
    plus_side = jnp.where(axis_kinds == 1, picked, first_partner)
    minus_parts = spread_faces(interp_table, own_faces)
    plus_parts = jnp.moveaxis(jnp.take(pool, axis_partners, axis=2), 2, 0)
    return (plus_side, minus_parts, plus_parts)


def surface_one(
    pool, own_faces, axis_kinds, axis_partners, axis_quadrants, direction, normal_sign, tables
):
    derivative, interp_table, project_table, edge_weight = tables
    plus_side, minus_parts, plus_parts = mortar_states(
        pool, own_faces, axis_kinds, axis_partners, axis_quadrants, interp_table
    )
    is_big = axis_kinds == 2

    def riemann(minus_side, plus_here):
        return face_flux(minus_side, plus_here, direction, normal_sign)

    def average(minus_side, plus_here):
        return 0.5 * (gradient_inputs(minus_side) + gradient_inputs(plus_here))

    def on_mortar(face_rule):
        return project_faces(project_table, jax.vmap(face_rule)(minus_parts, plus_parts))

    star_flux = jnp.where(is_big, on_mortar(riemann), riemann(own_faces, plus_side))
    inviscid = (star_flux - normal_sign * euler_flux(own_faces, direction)) / edge_weight
    star_vars = jnp.where(is_big, on_mortar(average), average(own_faces, plus_side))
    lifting = normal_sign * (star_vars - gradient_inputs(own_faces)) / edge_weight
    return (inviscid, lifting)


def surface_two(
    pool_flux, own_flux, axis_kinds, axis_partners, axis_quadrants, normal_sign, tables
):
    derivative, interp_table, project_table, edge_weight = tables
    plus_side, minus_parts, plus_parts = mortar_states(
        pool_flux, own_flux, axis_kinds, axis_partners, axis_quadrants, interp_table
    )
    mortar_mean = project_faces(project_table, 0.5 * normal_sign * (minus_parts + plus_parts))
    star_flux = jnp.where(axis_kinds == 2, mortar_mean, 0.5 * normal_sign * (own_flux + plus_side))
    return (star_flux - normal_sign * own_flux) / edge_weight


def local_gradients(conserved, metric, info_list, state_pools, tables):
    derivative = tables[0]
    elements = conserved.shape[-1]
    normal_sign = face_signs(elements)
    lifted_inputs = gradient_inputs(conserved)
    per_direction = []
    inviscid_list = []
    for d in range(3):
        own_faces = axis_traces(conserved, d)
        axis_kinds, axis_partners, axis_quadrants = info_list[d]
        inviscid, lifting = surface_one(
            state_pools[d],
            own_faces,
            axis_kinds,
            axis_partners,
            axis_quadrants,
            d,
            normal_sign,
            tables,
        )
        inviscid_list.append(inviscid)
        per_direction.append(add_faces(along_axis(lifted_inputs, derivative, d), d, lifting))
    gradients = jnp.stack(per_direction, axis=1).reshape(12, 5, 5, 5, elements) * metric
    return (gradients, inviscid_list)


def local_residual(
    conserved, metric, gradients, inviscid_list, own_fluxes, flux_pools, info_list, tables
):
    derivative = tables[0]
    elements = conserved.shape[-1]
    normal_sign = face_signs(elements)
    zero_row = jnp.zeros((1, 5, 5, 5, elements), jnp.float32)
    zero_face = jnp.zeros((1, 25, 2 * elements), jnp.float32)
    residual = jnp.zeros_like(conserved)
    for d in range(3):
        axis_kinds, axis_partners, axis_quadrants = info_list[d]
        viscous_face = surface_two(
            flux_pools[d],
            own_fluxes[d],
            axis_kinds,
            axis_partners,
            axis_quadrants,
            normal_sign,
            tables,
        )
        viscous_volume = along_axis(viscous_flux(conserved, gradients, d), derivative, d)
        change = jnp.concatenate([zero_row, viscous_volume], axis=0) - split_volume(
            conserved, derivative, d
        )
        change = add_faces(
            change, d, jnp.concatenate([zero_face, viscous_face], axis=0) - inviscid_list[d]
        )
        residual = residual + change
    return residual * metric


def pack_sub(own_lists, send_lists):
    picked = [jnp.take(own_lists[d], send_lists[:, d, :], axis=2) for d in range(3)]
    stacked = jnp.stack(picked, axis=3)
    return stacked.reshape(stacked.shape[0], 25, -1)


def pack_curve(own_lists, send_lists):
    picked = [
        jnp.take(own_lists[d], send_lists[r, d, :], axis=2) for r in range(2) for d in range(3)
    ]
    return jnp.concatenate(picked, axis=-1)


def assemble_pools(own_lists, arrived, curve_rim, peers, slots_sub, slots_curve):
    components = arrived.shape[0]
    sub_parts = arrived.reshape(components, 25, peers, 3, slots_sub)
    lower_part = curve_rim[:, :, : 3 * slots_curve].reshape(components, 25, 3, slots_curve)
    upper_part = curve_rim[:, :, 9 * slots_curve :].reshape(components, 25, 3, slots_curve)
    return [
        jnp.concatenate(
            [
                own_lists[d],
                sub_parts[:, :, :, d, :].reshape(components, 25, peers * slots_sub),
                lower_part[:, :, d, :],
                upper_part[:, :, d, :],
            ],
            axis=-1,
        )
        for d in range(3)
    ]


def share_states(own_lists, send_sub, send_curve):
    slots_curve = send_curve.shape[-1]
    arrived = lax.all_to_all(
        pack_sub(own_lists, send_sub), "sub", split_axis=2, concat_axis=2, tiled=True
    )
    curve_rim = extended(pack_curve(own_lists, send_curve), (("curve", 2),), 3 * slots_curve)
    return assemble_pools(
        own_lists, arrived, curve_rim, lax.axis_size("sub"), send_sub.shape[-1], slots_curve
    )


def share_gradients(own_lists, send_sub, send_curve):
    slots_curve = send_curve.shape[-1]
    arrived = lax.all_to_all(
        pack_sub(own_lists, send_sub), "sub", split_axis=2, concat_axis=2, tiled=True
    )
    curve_rim = extended(pack_curve(own_lists, send_curve), (("curve", 2),), 3 * slots_curve)
    return assemble_pools(
        own_lists, arrived, curve_rim, lax.axis_size("sub"), send_sub.shape[-1], slots_curve
    )


def local(
    state_now,
    section_memory,
    element_level,
    face_kind,
    face_partner,
    face_quadrant,
    send_sub,
    send_curve,
):
    tables = gl_tables()
    elements = state_now.shape[-1]
    conserved = state_now.reshape(5, 5, 5, 5, elements)
    metric = 1.0 + element_level.astype(jnp.float32)
    info_list = [axis_info(face_kind, face_partner, face_quadrant, d) for d in range(3)]
    own_states = [axis_traces(conserved, d) for d in range(3)]
    state_pools = share_states(own_states, send_sub, send_curve)
    gradients, inviscid_list = local_gradients(conserved, metric, info_list, state_pools, tables)
    own_gradients = [axis_traces(gradients, d) for d in range(3)]
    gradient_pools = share_gradients(own_gradients, send_sub, send_curve)
    flux_pools = [viscous_flux(state_pools[d], gradient_pools[d], d) for d in range(3)]
    own_fluxes = [flux_pools[d][:, :, : 2 * elements] for d in range(3)]
    residual = local_residual(
        conserved, metric, gradients, inviscid_list, own_fluxes, flux_pools, info_list, tables
    )
    memory_next = section_decay * section_memory + time_step * residual.reshape(5, 125, elements)
    state_next = state_now + section_weight * memory_next
    return (state_next, memory_next)


def solution(mesh):
    placed = (
        P(None, None, ("curve", "sub")),
        P(None, None, ("curve", "sub")),
        P(("curve", "sub")),
        P(None, ("curve", "sub")),
        P(None, None, ("curve", "sub")),
        P(None, ("curve", "sub")),
        P(("curve", "sub"), None, None),
        P(("curve", "sub"), None, None),
    )
    return jax.shard_map(
        local,
        mesh=mesh,
        in_specs=placed,
        out_specs=(P(None, None, ("curve", "sub")), P(None, None, ("curve", "sub"))),
        check_vma=False,
    )
```

profile of v0, /device:TPU:1, one launch (start us, length us, event | category | flops | bytes accessed | tf_op | source)
XLA Modules:
  0.0 432.8 jit_solution(11976724635292535932)
XLA Ops:
  11.3 14.4 %all-to-all-start = ((f32[8,1,1500]{2,1,0:T(1,128)}), f32[8,1,1500]{2,1,0:T(1,128)}, u32[]{:S(2)}, u32[]{:S(2)}) async-start(f32[8,1,1500]{2,1,0:T(1,128)} %reshape.19298), calls=%async_computation | async-start | bytes 98304 | tf_op jit(solution)/shard_map/all_to_all | solution.py:361
  37.8 8.8 %collective-permute-start.1 = (f32[5,25,96]{2,1,0:T(8,128)}, f32[5,25,96]{2,1,0:T(8,128)}, u32[]{:S(2)}, u32[]{:S(2)}) collective-permute-start(f32[5,25,96]{2,1,0:T(8,128)} %pad_maximum_fusion.18), channel_id=1, source_target_pairs={{8,0},{16,8},{24,16},{32,24},{40,32},{48,40},{56,48},{64,56},{72,6... | collective-permute-start | bytes 144008 | tf_op jit(solution)/shard_map/ppermute | solution.py:26
  100.5 9.6 %gather_fusion.9 = f32[1024,5,25]{2,1,0:T(8,128)} fusion(f32[5,25,352]{1,0,2:T(8,128)} %copy.8293, s32[1024]{0:T(1024)S(1)} %broadcast_clamp_fusion.2), kind=kCustom, calls=%fused_computation.2.clone | custom fusion | bytes 1028096 | tf_op jit(solution)/shard_map/jit(_take)/gather | solution.py:229
  110.1 3.4 copy.8295
  123.4 9.7 %gather_fusion.11 = f32[1024,5,25]{2,1,0:T(8,128)} fusion(f32[5,25,352]{1,0,2:T(8,128)} %copy.8306, s32[1024]{0:T(1024)} %get-tuple-element.864), kind=kCustom, calls=%fused_computation.15.clone | custom fusion | bytes 1028096 | tf_op jit(solution)/shard_map/jit(_take)/gather | solution.py:229
  133.1 3.4 copy.8308
  145.6 9.7 %gather_fusion.13 = f32[1024,5,25]{2,1,0:T(8,128)} fusion(f32[5,25,352]{1,0,2:T(8,128)} %copy.8319, s32[1024]{0:T(1024)} %get-tuple-element.863), kind=kCustom, calls=%fused_computation.16.clone | custom fusion | bytes 1028096 | tf_op jit(solution)/shard_map/jit(_take)/gather | solution.py:229
  155.4 3.6 copy.8321
  162.5 3.2 gather_fusion.14
  182.3 3.2 gather_fusion.12
  200.0 3.2 gather_fusion.10
  224.4 3.1 pad_maximum_fusion.2
  230.4 3.0 gather_fusion.20
  238.1 3.0 pad_maximum_fusion.1
  241.2 3.2 gather_fusion.16
  244.4 3.0 gather_fusion.19
  252.1 3.1 pad_maximum_fusion
  264.1 3.0 gather_fusion.22
  298.1 5.2 %all-to-all-start.1 = ((f32[8,1,3600]{2,1,0:T(1,128)}), f32[8,1,3600]{2,1,0:T(1,128)}, u32[]{:S(2)}, u32[]{:S(2)}) async-start(f32[8,1,3600]{2,1,0:T(1,128)} %reshape.19300), calls=%async_computation.1 | async-start | bytes 237568 | tf_op jit(solution)/shard_map/all_to_all | solution.py:372
  311.5 7.0 %collective-permute-start.3 = (f32[12,25,96]{2,1,0:T(8,128)}, f32[12,25,96]{2,1,0:T(8,128)}, u32[]{:S(2)}, u32[]{:S(2)}) collective-permute-start(f32[12,25,96]{2,1,0:T(8,128)} %pad_maximum_fusion.10), channel_id=1, source_target_pairs={{8,0},{16,8},{24,16},{32,24},{40,32},{48,40},{56,48},{64,56},{72,6... | collective-permute-start | bytes 345608 | tf_op jit(solution)/shard_map/ppermute | solution.py:26
  354.9 8.2 %gather_fusion.28 = f32[1024,4,25]{2,1,0:T(4,128)} fusion(f32[4,25,352]{1,0,2:T(4,128)S(1)} %copy.8615, s32[1024]{0:T(1024)S(1)} %copy-done.296), kind=kCustom, calls=%fused_computation.27.clone | custom fusion | bytes 823296 | tf_op jit(solution)/shard_map/jit(_take)/gather | solution.py:229
  370.1 8.0 %gather_fusion.26 = f32[1024,4,25]{2,1,0:T(4,128)} fusion(f32[4,25,352]{1,0,2:T(4,128)S(1)} %copy.8502, s32[1024]{0:T(1024)S(1)} %copy-done.295), kind=kCustom, calls=%fused_computation.26.clone | custom fusion | bytes 823296 | tf_op jit(solution)/shard_map/jit(_take)/gather | solution.py:229
  381.5 4.7 %gather_fusion.24 = f32[1024,4,25]{2,1,0:T(4,128)S(1)} fusion(f32[4,25,352]{1,0,2:T(4,128)} %copy.8460, s32[1024]{0:T(1024)S(1)} %copy-done.292), kind=kCustom, calls=%fused_computation.6.clone | custom fusion | bytes 823296 | tf_op jit(solution)/shard_map/jit(_take)/gather | solution.py:229
  386.2 3.0 gather_fusion.25
  (1270 shorter events, 295.9 us)
Async XLA Ops:
  3.4 83.9 %copy-start.17 = (f32[5,25,256]{2,1,0:T(8,128)}, f32[5,25,256]{2,1,0:T(8,128)S(1)}, u32[]{:S(2)}) copy-start(f32[5,25,256]{2,1,0:T(8,128)S(1)} %constant_dynamic-update-slice_fusion.9) | copy-start | bytes 384004
  3.8 22.5 %copy-start.321 = (pred[32]{0:T(512)(128)(4,1)}, pred[32]{0:T(512)(128)(4,1)S(1)}, u32[]{:S(2)}) copy-start(pred[32]{0:T(512)(128)(4,1)S(1)} %get-tuple-element.836) | copy-start | bytes 100
  3.8 23.3 %copy-start.319 = (pred[32]{0:T(512)(128)(4,1)}, pred[32]{0:T(512)(128)(4,1)S(1)}, u32[]{:S(2)}) copy-start(pred[32]{0:T(512)(128)(4,1)S(1)} %get-tuple-element.838) | copy-start | bytes 100
  3.9 25.3 %copy-start.317 = (pred[32]{0:T(512)(128)(4,1)}, pred[32]{0:T(512)(128)(4,1)S(1)}, u32[]{:S(2)}) copy-start(pred[32]{0:T(512)(128)(4,1)S(1)} %get-tuple-element.840) | copy-start | bytes 100
  3.9 30.0 %copy-start.315 = (pred[32]{0:T(512)(128)(4,1)}, pred[32]{0:T(512)(128)(4,1)S(1)}, u32[]{:S(2)}) copy-start(pred[32]{0:T(512)(128)(4,1)S(1)} %get-tuple-element.842) | copy-start | bytes 100
  3.9 30.9 %copy-start.313 = (pred[32]{0:T(512)(128)(4,1)}, pred[32]{0:T(512)(128)(4,1)S(1)}, u32[]{:S(2)}) copy-start(pred[32]{0:T(512)(128)(4,1)S(1)} %get-tuple-element.844) | copy-start | bytes 100
  3.9 32.9 %copy-start.311 = (pred[32]{0:T(512)(128)(4,1)}, pred[32]{0:T(512)(128)(4,1)S(1)}, u32[]{:S(2)}) copy-start(pred[32]{0:T(512)(128)(4,1)S(1)} %get-tuple-element.427) | copy-start | bytes 100
  4.1 23.3 %copy-start.305 = (s32[1024]{0:T(1024)}, s32[1024]{0:T(1024)S(1)}, u32[]{:S(2)}) copy-start(s32[1024]{0:T(1024)S(1)} %get-tuple-element.859) | copy-start | bytes 12292
  4.9 189.0 %copy-start.13 = (f32[5,25,256]{2,1,0:T(8,128)}, f32[5,25,256]{2,1,0:T(8,128)S(1)}, u32[]{:S(2)}) copy-start(f32[5,25,256]{2,1,0:T(8,128)S(1)} %constant_dynamic-update-slice_fusion.7) | copy-start | bytes 384004
  6.5 203.2 %copy-start.15 = (f32[5,25,256]{2,1,0:T(8,128)}, f32[5,25,256]{2,1,0:T(8,128)S(1)}, u32[]{:S(2)}) copy-start(f32[5,25,256]{2,1,0:T(8,128)S(1)} %constant_dynamic-update-slice_fusion.5) | copy-start | bytes 384004
  10.1 22.0 %copy-start.231 = (s32[4,6,128]{2,0,1:T(4,128)S(1)}, s32[4,6,128]{2,0,1:T(4,128)}, u32[]{:S(2)}) copy-start(s32[4,6,128]{2,0,1:T(4,128)} %param.78) | copy-start | bytes 36868
  11.3 79.0 %all-to-all-start = ((f32[8,1,1500]{2,1,0:T(1,128)}), f32[8,1,1500]{2,1,0:T(1,128)}, u32[]{:S(2)}, u32[]{:S(2)}) async-start(f32[8,1,1500]{2,1,0:T(1,128)} %reshape.19298), calls=%async_computation | async-start | bytes 98304 | tf_op jit(solution)/shard_map/all_to_all | solution.py:361
  26.4 20.2 %copy-start.31 = (f32[5,125,128]{2,1,0:T(8,128)S(1)}, f32[5,125,128]{2,1,0:T(8,128)}, u32[]{:S(2)}) copy-start(f32[5,125,128]{2,1,0:T(8,128)} %param.74) | copy-start | bytes 960004
  30.2 64.0 %collective-permute-start = (f32[5,25,96]{2,1,0:T(8,128)}, f32[5,25,96]{2,1,0:T(8,128)}, u32[]{:S(2)}, u32[]{:S(2)}) collective-permute-start(f32[5,25,96]{2,1,0:T(8,128)} %pad_maximum_fusion.17), channel_id=1, source_target_pairs={{0,8},{8,16},{16,24},{24,32},{32,40},{40,48},{48,56},{56,64},{64,7... | collective-permute-start | bytes 144008 | tf_op jit(solution)/shard_map/ppermute | solution.py:24
  33.3 29.7 %copy-start.308 = (s32[1024]{0:T(1024)}, s32[1024]{0:T(1024)S(1)}, u32[]{:S(2)}) copy-start(s32[1024]{0:T(1024)S(1)} %get-tuple-element.854) | copy-start | bytes 12292
  34.1 29.7 %copy-start.309 = (s32[1024]{0:T(1024)}, s32[1024]{0:T(1024)S(1)}, u32[]{:S(2)}) copy-start(s32[1024]{0:T(1024)S(1)} %get-tuple-element.856) | copy-start | bytes 12292
  34.2 29.7 %copy-start.310 = (s32[1024]{0:T(1024)}, s32[1024]{0:T(1024)S(1)}, u32[]{:S(2)}) copy-start(s32[1024]{0:T(1024)S(1)} %get-tuple-element.855) | copy-start | bytes 12292
  37.8 58.2 %collective-permute-start.1 = (f32[5,25,96]{2,1,0:T(8,128)}, f32[5,25,96]{2,1,0:T(8,128)}, u32[]{:S(2)}, u32[]{:S(2)}) collective-permute-start(f32[5,25,96]{2,1,0:T(8,128)} %pad_maximum_fusion.18), channel_id=1, source_target_pairs={{8,0},{16,8},{24,16},{32,24},{40,32},{48,40},{56,48},{64,56},{72,6... | collective-permute-start | bytes 144008 | tf_op jit(solution)/shard_map/ppermute | solution.py:26
  90.3 120.2 %copy-start.229 = (f32[256]{0:T(256)}, f32[256]{0:T(256)S(1)}, u32[]{:S(2)}) copy-start(f32[256]{0:T(256)S(1)} %get-tuple-element.871) | copy-start | bytes 3076
  114.6 82.9 %copy-start.3 = (f32[4,5,25,256]{3,2,0,1:T(8,128)}, f32[4,5,25,256]{3,2,0,1:T(8,128)S(1)}, u32[]{:S(2)}) copy-start(f32[4,5,25,256]{3,2,0,1:T(8,128)S(1)} %select_bitcast_fusion.2) | copy-start | bytes 1536004
  293.9 40.7 %copy-start.40 = (f32[4,5,25,256]{3,2,0,1:T(8,128)}, f32[4,5,25,256]{3,2,0,1:T(8,128)S(1)}, u32[]{:S(2)}) copy-start(f32[4,5,25,256]{3,2,0,1:T(8,128)S(1)} %get-tuple-element.846) | copy-start | bytes 1536004
  298.1 45.4 %all-to-all-start.1 = ((f32[8,1,3600]{2,1,0:T(1,128)}), f32[8,1,3600]{2,1,0:T(1,128)}, u32[]{:S(2)}, u32[]{:S(2)}) async-start(f32[8,1,3600]{2,1,0:T(1,128)} %reshape.19300), calls=%async_computation.1 | async-start | bytes 237568 | tf_op jit(solution)/shard_map/all_to_all | solution.py:372
  307.6 38.8 %collective-permute-start.2 = (f32[12,25,96]{2,1,0:T(8,128)}, f32[12,25,96]{2,1,0:T(8,128)}, u32[]{:S(2)}, u32[]{:S(2)}) collective-permute-start(f32[12,25,96]{2,1,0:T(8,128)} %pad_maximum_fusion.9), channel_id=1, source_target_pairs={{0,8},{8,16},{16,24},{24,32},{32,40},{40,48},{48,56},{56,64},{64,7... | collective-permute-start | bytes 345608 | tf_op jit(solution)/shard_map/ppermute | solution.py:24
  311.5 37.9 %collective-permute-start.3 = (f32[12,25,96]{2,1,0:T(8,128)}, f32[12,25,96]{2,1,0:T(8,128)}, u32[]{:S(2)}, u32[]{:S(2)}) collective-permute-start(f32[12,25,96]{2,1,0:T(8,128)} %pad_maximum_fusion.10), channel_id=1, source_target_pairs={{8,0},{16,8},{24,16},{32,24},{40,32},{48,40},{56,48},{64,56},{72,6... | collective-permute-start | bytes 345608 | tf_op jit(solution)/shard_map/ppermute | solution.py:26
  (332 other events, 1482.3 us)
where the time goes:
time: 441 us; the launch traced here: 433 us
  local copies, waits for them, and re-layouts  243 us (55%)
  other arithmetic  100 us (23%)
  matrix products  43.2 us (10%)
  starting transfers between devices  39.3 us (9%)
  between operations  7.16 us (2%)
    gather x12, local copies, waits for them, and re-layouts, mortar_states(): plus_parts = jnp.moveaxis(jnp.take(pool, axis_partners, axis=2), 2, 0)  67.1 us
    dot_general x36, matrix products, project_faces(): jnp.tensordot(project_table[q], parts[q], axes=([1], [1]), precision=high...  27.8 us
    unnamed x741, local copies, waits for them, and re-layouts  26.8 us
    gather x12, local copies, waits for them, and re-layouts, mortar_states(): first_partner = jnp.take(pool, axis_partners[0], axis=2)  26.2 us
    gather x12, local copies, waits for them, and re-layouts, pack_curve(): jnp.take(own_lists[d], send_lists[r, d, :], axis=2)  23.9 us
    unnamed x105, other arithmetic  19 us
    reshape x18, local copies, waits for them, and re-layouts, face_trace(): return picked.reshape(picked.shape[0], 25, picked.shape[-1])  16.8 us
    mul x30, local copies, waits for them, and re-layouts, split_volume(): 0.5 * (rho_s[i] + rho_s[m]) * (0.5 * (normal_s[i] + normal_s[m]))  16.2 us
  transfers between devices with their start and end apart: 6, of which 0 were waited for; matrix products, arithmetic and copies ran while one was open for 21% of the time, Pallas kernels for 0%

commit v1 on v0

v1 whole, which is shorter than its diff:
```python
import functools
import math

import jax
import jax.numpy as jnp
import ml_dtypes
import numpy as np
from jax import lax
from jax.experimental import pallas as pl
from jax.experimental.pallas import tpu as pltpu
from jax.sharding import PartitionSpec as P

viscosity = 0.1
conduction = 0.1 * 1.4 / (0.4 * 0.72)
time_step = 0.02
section_decay = -567301805773.0 / 1357537059087.0
section_weight = 5161836677717.0 / 13612068292357.0
EDGE = 0.1
F32, BF16 = jnp.float32, jnp.bfloat16
ELEMENTS = 128
VMEM_LIMIT = 56 * 1024 * 1024


def node_tables():
    nodes = np.array([-1.0, -math.sqrt(3.0 / 7.0), 0.0, math.sqrt(3.0 / 7.0), 1.0])
    weights = np.array([0.1, 49.0 / 90.0, 32.0 / 45.0, 49.0 / 90.0, 0.1])
    prods = np.array(
        [np.prod([nodes[m] - nodes[k] for k in range(5) if k != m]) for m in range(5)]
    )
    deriv = np.zeros((5, 5))
    for i in range(5):
        for m in range(5):
            if i != m:
                deriv[i, m] = prods[i] / prods[m] / (nodes[i] - nodes[m])
        deriv[i, i] = -np.sum(deriv[i])

    def lagrange(points):
        values = np.ones((5, 5))
        for m in range(5):
            for k in range(5):
                if k != m:
                    values[:, m] = values[:, m] * (points - nodes[k]) / (nodes[m] - nodes[k])
        return values

    halves = [lagrange((nodes - 1.0) / 2.0), lagrange((nodes + 1.0) / 2.0)]
    projs = [0.5 * (h * weights[:, None]).T / weights[:, None] for h in halves]
    interp = [np.kron(halves[a], halves[b]) for a in range(2) for b in range(2)]
    project = [np.kron(projs[a], projs[b]) for a in range(2) for b in range(2)]
    return deriv, interp, project


def padded(matrix, rows, cols):
    out = np.zeros((rows, cols))
    out[: matrix.shape[0], : matrix.shape[1]] = matrix
    return out


def split_np(matrix):
    high = matrix.astype(np.float32).astype(ml_dtypes.bfloat16)
    low = (matrix - high.astype(np.float64)).astype(np.float32).astype(ml_dtypes.bfloat16)
    return high, low


def stack3(matrix):
    high, low = split_np(matrix)
    return np.concatenate([high, high, low], axis=1)


@functools.lru_cache(maxsize=None)
def constants():
    deriv, interp, project = node_tables()
    eye5 = np.eye(5)
    big = [
        np.kron(np.kron(eye5, eye5), deriv),
        np.kron(np.kron(eye5, deriv), eye5),
        np.kron(np.kron(deriv, eye5), eye5),
    ]
    index = np.arange(125)
    coord = [index % 5, (index // 5) % 5, index // 25]
    trace = {}
    for d in range(3):
        for s in range(2):
            rows = index[coord[d] == 4 * s]
            t = np.zeros((25, 125))
            t[np.arange(25), rows] = 1.0
            trace[d, s] = t
    sigma = (-1.0, 1.0)
    edge_sign = [
        sum(sigma[s] / EDGE * trace[d, s].T @ trace[d, s] for s in range(2)) for d in range(3)
    ]
    out = {}
    out["deriv_all"] = stack3(np.concatenate([padded(big[d], 128, 128) for d in range(3)], axis=0))
    out["deriv_sum"] = np.concatenate([stack3(padded(big[d], 128, 128)) for d in range(3)], axis=1)
    out["own"] = np.stack(
        [
            np.concatenate(
                [
                    stack3(padded(m @ trace[d, s], 32, 128))
                    for s in range(2)
                    for m in [np.eye(25)] + interp
                ],
                axis=0,
            )
            for d in range(3)
        ]
    )
    spread = np.zeros((160, 128))
    for c in range(5):
        spread[c * 32 : c * 32 + 25, c * 25 : c * 25 + 25] = np.eye(25)
    out["spread"] = spread.astype(ml_dtypes.bfloat16)
    out["quads"] = stack3(np.concatenate([padded(interp[q], 32, 32) for q in range(4)], axis=0))
    out["lift"] = np.stack(
        [
            stack3(
                np.concatenate(
                    [
                        padded(0.5 / EDGE * trace[d, s].T @ m, 128, 32)
                        for s in range(2)
                        for m in project + [np.eye(25)]
                    ],
                    axis=1,
                )
            )
            for d in range(3)
        ]
    )

    def packer(comps, d):
        m = np.zeros((256, comps * 128))
        for s in range(2):
            for c in range(comps):
                m[s * 128 + c * 25 : s * 128 + c * 25 + 25, c * 128 : c * 128 + 125] = trace[d, s]
        return m.astype(ml_dtypes.bfloat16)

    out["pack_state"] = np.stack([packer(5, d) for d in range(3)])
    out["pack_flux"] = np.stack([packer(4, d) for d in range(3)])
    both = sum(project[q] @ interp[q] for q in range(4))
    own_visc = []
    for d in range(3):
        own_visc.append(stack3(padded(big[d] - 0.5 * edge_sign[d], 128, 128)))
        own_visc.append(
            stack3(
                padded(
                    sum(
                        0.5 * sigma[s] / EDGE * trace[d, s].T @ (both - np.eye(25)) @ trace[d, s]
                        for s in range(2)
                    ),
                    128,
                    128,
                )
            )
        )
    out["own_visc"] = np.concatenate(own_visc, axis=1)
    out["face_rows"] = np.stack(
        [
            np.concatenate([padded(trace[d, s], 32, 128) for s in range(2)], axis=0)
            for d in range(3)
        ]
    ).astype(ml_dtypes.bfloat16)
    out["visc"] = np.stack(
        [
            stack3(
                np.concatenate(
                    [
                        padded(0.5 * sigma[s] / EDGE * trace[d, s].T @ m, 128, 32)
                        for s in range(2)
                        for m in [np.eye(25)] + interp + project
                    ],
                    axis=1,
                )
            )
            for d in range(3)
        ]
    )
    signs = np.zeros((3, 128, 128), np.float32)
    for d in range(3):
        signs[d, :125, :] = np.diag(edge_sign[d])[:, None]
    out["signs"] = signs
    return out


def split(x):
    high = x.astype(BF16)
    return high, (x - high.astype(F32)).astype(BF16)


def dot(a, b):
    return lax.dot_general(a, b, (((1,), (0,)), ((), ())), preferred_element_type=F32)


def dot_nt(a, b):
    return lax.dot_general(a, b, (((1,), (1,)), ((), ())), preferred_element_type=F32)


def lanes(parts):
    return jnp.concatenate(parts, axis=1)


def rows(parts):
    return jnp.concatenate(parts, axis=0)


def one_hot(index_row, count):
    width = index_row.shape[1]
    numbers = lax.broadcasted_iota(jnp.int32, (count, width), 0)
    return jnp.where(numbers == index_row, 1.0, 0.0).astype(BF16)


def load_padded(ref, pad, count):
    for c in range(count):
        pad[c, 120:128, :] = jnp.full((8, ELEMENTS), 1.0 if c in (0, 4) else 0.0, F32)
        pad[c, 0:125, :] = ref[c]


def point_values(u):
    inverse = 1.0 / u[0]
    vel = [u[1 + k] * inverse for k in range(3)]
    kinetic = u[1] * vel[0] + u[2] * vel[1] + u[3] * vel[2]
    pressure = 0.4 * (u[4] - 0.5 * kinetic)
    return inverse, vel, pressure


def send_pack(high, low, pick_ref, outs):
    data = rows([lanes(high), lanes(low)])
    for t in range(3):
        hot = rows([one_hot(pick_ref[t, d : d + 1, :], 256) for d in range(3)])
        both = dot(data, hot)
        block = both[0:128] + both[128:256]
        outs[t][...] = jnp.transpose(block)[0 : outs[t].shape[0]]


def pack_kernel(state_ref, pick_ref, pack_ref, sub_ref, first_ref, second_ref, pad):
    load_padded(state_ref, pad, 5)
    parts = [split(pad[c]) for c in range(5)]
    right = rows([lanes([h, l]) for h, l in parts])
    high, low = [], []
    for d in range(3):
        both = dot(pack_ref[d], right).astype(BF16)
        high.append(lanes([both[0:128, 0:128], both[128:256, 0:128]]))
        low.append(lanes([both[0:128, 128:256], both[128:256, 128:256]]))
    send_pack(high, low, pick_ref, (sub_ref, first_ref, second_ref))


def volume_kernel(state_ref, all_ref, sum_ref, sign_ref, vol_ref, grad_ref, pad, res):
    load_padded(state_ref, pad, 5)
    u = [pad[c] for c in range(5)]
    inverse, vel, pressure = point_values(u)
    total = u[4] + pressure
    enthalpy = total * inverse
    temperature = pressure * inverse
    fields = [u[0], vel[0], vel[1], vel[2], u[1], u[2], u[3], enthalpy, total, temperature]
    for f, value in enumerate(fields):
        h, l = split(value)
        res[:, f * 128 : (f + 1) * 128] = dot(all_ref[...], rows([h, l, h]))

    def der(f, d):
        return res[d * 128 : (d + 1) * 128, f * 128 : (f + 1) * 128]

    for d in range(3):
        for v, f in enumerate((1, 2, 3, 9)):
            grad_ref[3 * v + d] = der(f, d) - sign_ref[d] * fields[f]
    div_vel = der(1, 0) + der(2, 1) + der(3, 2)
    div_mom = der(4, 0) + der(5, 1) + der(6, 2)
    advect = vel[0] * der(0, 0) + vel[1] * der(0, 1) + vel[2] * der(0, 2)
    carry = advect + div_mom
    mass = 0.5 * (u[0] * div_vel + carry)
    edge_mass = sign_ref[0] * u[1] + sign_ref[1] * u[2] + sign_ref[2] * u[3]
    vol_ref[0] = edge_mass - mass
    specific = [vel[0], vel[1], vel[2], enthalpy]
    full = [u[1], u[2], u[3], total]
    for k in range(4):
        cross = []
        direct = []
        edge = None
        for d in range(3):
            product = full[k] * vel[d]
            flux = product + pressure if k == d else product
            edge_d = sign_ref[d] * flux
            edge = edge_d if edge is None else edge + edge_d
            h, l = split(specific[k] * vel[d])
            cross += [h, l, h]
            h, l = split(product + 4.0 * pressure if k == d else product)
            direct += [h, l, h]
        both = dot(sum_ref[...], lanes([rows(cross), rows(direct)]))
        f_spec, f_full = (1 + k, 4 + k) if k < 3 else (7, 8)
        quad = full[k] * div_vel + specific[k] * carry + u[0] * both[:, 0:128] + both[:, 128:256]
        for d in range(3):
            quad = quad + u[1 + d] * der(f_spec, d) + vel[d] * der(f_full, d)
        vol_ref[1 + k] = edge - 0.25 * quad


def partner_rows(index, d):
    peer = 256 + lax.shift_right_logical(index - 256, 2) * 16 + (index & 3) + 4 * d
    return jnp.where(index < 256, index, jnp.where(index < 288, peer, index + 96))


def gather_hot(partner_ref, kind_ref, parity, d):
    blocks = []
    for q in range(4):
        for s in range(2):
            f = 2 * d + s
            index = partner_ref[q, f : f + 1, :]
            index = jnp.where(index >= 288, swap_curve(index, parity), index)
            row = partner_rows(index, d)
            if q > 0:
                row = jnp.where(kind_ref[f : f + 1, :] == 2, row, -1)
            blocks.append(one_hot(row, 448))
    return lanes(blocks)


def swap_curve(index, parity):
    other = jnp.where(index < 320, index + 32, index - 32)
    return jnp.where(parity == 0, other, index)


def remote_pool(sub_ref, first_ref, second_ref, spread, d):
    arrived = rows(
        [sub_ref[...], first_ref[32 * d : 32 * d + 32, :], second_ref[32 * d : 32 * d + 32, :]]
    )
    h, l = split(arrived)
    return dot_nt(spread, h).astype(BF16), dot_nt(spread, l).astype(BF16)


def surface_kernel(
    parity_ref,
    state_ref,
    grad_in_ref,
    vol_ref,
    level_ref,
    kind_ref,
    partner_ref,
    quadrant_ref,
    sub_ref,
    first_ref,
    second_ref,
    pick_ref,
    own_ref,
    spread_ref,
    quads_ref,
    lift_ref,
    pack_ref,
    acc_ref,
    flux_ref,
    sub_out,
    first_out,
    second_out,
    pad,
    own,
    got,
    quad,
    grad,
):
    parity = parity_ref[0]
    load_padded(state_ref, pad, 5)
    parts = [split(pad[c]) for c in range(5)]
    high = lanes([h for h, l in parts])
    low = lanes([l for h, l in parts])
    right = rows([high, low, high])
    metric = 1.0 + level_ref[...].astype(F32)
    spare = jnp.where(
        lax.broadcasted_iota(jnp.int32, (32, ELEMENTS), 0) >= 25, 1.0, 0.0
    ).astype(F32)
    acc = [vol_ref[c] for c in range(5)]
    for c in range(5):
        acc_ref[c] = vol_ref[c]
    for d in range(3):
        own[...] = dot(own_ref[d], right)
        pool_h, pool_l = [], []
        for s in range(2):
            h, l = split(own[s * 160 : s * 160 + 32, :])
            pool_h.append(rows([h[:, c * 128 : (c + 1) * 128] for c in range(5)]))
            pool_l.append(rows([l[:, c * 128 : (c + 1) * 128] for c in range(5)]))
        far_h, far_l = remote_pool(sub_ref, first_ref, second_ref, spread_ref[...], d)
        pool = rows([lanes(pool_h + [far_h]), lanes(pool_l + [far_l])])
        hot = gather_hot(partner_ref, kind_ref, parity, d)
        both = dot(pool, hot)
        got[...] = both[0:160] + both[160:320]
        parts = [split(got[c * 32 : (c + 1) * 32, 0:256]) for c in range(5)]
        first_h = lanes([h for h, l in parts])
        first_l = lanes([l for h, l in parts])
        quad[...] = dot(quads_ref[...], rows([first_h, first_l, first_h]))
        stacks = {}
        for s in range(2):
            f = 2 * d + s
            sign = 2 * s - 1
            kind = jnp.broadcast_to(kind_ref[f : f + 1, :], (32, ELEMENTS))
            quarter = jnp.broadcast_to(quadrant_ref[f : f + 1, :], (32, ELEMENTS))
            is_big = kind == 2
            is_small = kind == 1
            for q in range(4):
                left, far = [], []
                for c in range(5):
                    spot = slice(c * 128, (c + 1) * 128)
                    minus = own[s * 160 + 32 * (q + 1) : s * 160 + 32 * (q + 2), spot]
                    plus = got[
                        c * 32 : (c + 1) * 32, q * 256 + s * 128 : q * 256 + (s + 1) * 128
                    ]
                    if q == 0:
                        minus = jnp.where(is_big, minus, own[s * 160 : s * 160 + 32, spot])
                        wide = slice(c * 256 + s * 128, c * 256 + (s + 1) * 128)
                        part = quad[96:128, wide]
                        for t in (2, 1, 0):
                            part = jnp.where(quarter == t, quad[32 * t : 32 * t + 32, wide], part)
                        plus = jnp.where(is_small, part, plus)
                    if c in (0, 4):
                        minus = minus + spare
                        plus = plus + spare
                    left.append(minus)
                    far.append(plus)
                if q > 0:
                    far[0] = jnp.where(is_big, far[0], 1.0)
                inv_l, vel_l, press_l = point_values(left)
                inv_r, vel_r, press_r = point_values(far)
                temp_l, temp_r = press_l * inv_l, press_r * inv_r
                speed = jnp.maximum(
                    jnp.abs(vel_l[d]) + jnp.sqrt(1.4 * temp_l),
                    jnp.abs(vel_r[d]) + jnp.sqrt(1.4 * temp_r),
                )
                values = []
                for c in range(5):
                    if c == 0:
                        central = left[1 + d] + far[1 + d]
                    elif c == 4:
                        central = (left[4] + press_l) * vel_l[d] + (far[4] + press_r) * vel_r[d]
                    else:
                        central = left[c] * vel_l[d] + far[c] * vel_r[d]
                        if c == 1 + d:
                            central = central + (press_l + press_r)
                    jump = speed * (far[c] - left[c])
                    values.append(jump - central if sign > 0 else jump + central)
                for a, b in zip(vel_l + [temp_l], vel_r + [temp_r]):
                    values.append(a + b if sign > 0 else -a - b)
                picked = [split(jnp.where(is_big, v, 0.0)) for v in values]
                stacks[s, q] = [lanes([p[j] for p in picked]) for j in range(2)]
                if q == 0:
                    plain = [split(jnp.where(is_big, 0.0, v)) for v in values]
                    stacks[s, 4] = [lanes([p[j] for p in plain]) for j in range(2)]
        stack_h = rows([stacks[s, b][0] for s in range(2) for b in range(5)])
        stack_l = rows([stacks[s, b][1] for s in range(2) for b in range(5)])
        lifted = dot(lift_ref[d], rows([stack_h, stack_l, stack_h]))
        for c in range(5):
            acc_ref[c] = acc_ref[c] + lifted[:, c * 128 : (c + 1) * 128]
        for v in range(4):
            grad[3 * v + d] = metric * (
                grad_in_ref[3 * v + d] + lifted[:, (5 + v) * 128 : (6 + v) * 128]
            )
    inverse = 1.0 / pad[0]
    vel = [pad[1 + k] * inverse for k in range(3)]
    divergence = (2.0 / 3.0 * viscosity) * (grad[0] + grad[4] + grad[8])
    for d in range(3):
        heat = conduction * grad[9 + d]
        for k in range(3):
            tau = viscosity * (grad[3 * d + k] + grad[3 * k + d])
            if k == d:
                tau = tau - divergence
            flux_ref[d, k] = tau
            heat = heat + vel[k] * tau
        flux_ref[d, 3] = heat
    high, low = [], []
    for d in range(3):
        right = rows([lanes(list(split(flux_ref[d, c]))) for c in range(4)])
        both = dot(pack_ref[d], right).astype(BF16)
        high.append(lanes([both[0:128, 0:128], both[128:256, 0:128]]))
        low.append(lanes([both[0:128, 128:256], both[128:256, 128:256]]))
    send_pack(high, low, pick_ref, (sub_out, first_out, second_out))


def own_viscous_kernel(flux_ref, acc_in_ref, kind_ref, matrix_ref, acc_ref):
    numbers = lax.broadcasted_iota(jnp.int32, (128, ELEMENTS), 0)
    places = (numbers % 5, (numbers // 5) % 5, numbers // 25)
    parts = []
    for d in range(3):
        at = places[d]
        low_big = jnp.broadcast_to(kind_ref[2 * d : 2 * d + 1, :], (128, ELEMENTS)) == 2
        high_big = jnp.broadcast_to(kind_ref[2 * d + 1 : 2 * d + 2, :], (128, ELEMENTS)) == 2
        big = ((at == 0) & low_big) | ((at == 4) & high_big)
        plain = [split(flux_ref[d, c]) for c in range(4)]
        masked = [split(jnp.where(big, flux_ref[d, c], 0.0)) for c in range(4)]
        for group in (plain, masked):
            h = lanes([p[0] for p in group])
            l = lanes([p[1] for p in group])
            parts += [h, l, h]
    both = dot(matrix_ref[...], rows(parts))
    acc_ref[0] = acc_in_ref[0]
    for c in range(4):
        acc_ref[1 + c] = acc_in_ref[1 + c] + both[:, c * 128 : (c + 1) * 128]


def final_kernel(
    parity_ref,
    state_ref,
    memory_ref,
    level_ref,
    kind_ref,
    partner_ref,
    quadrant_ref,
    flux_ref,
    acc_in_ref,
    sub_ref,
    first_ref,
    second_ref,
    faces_ref,
    spread_ref,
    visc_ref,
    state_out,
    memory_out,
    acc,
):
    parity = parity_ref[0]
    for d in range(3):
        parts = [split(flux_ref[d, c]) for c in range(4)]
        traces = dot(
            faces_ref[d], lanes([p[0] for p in parts] + [p[1] for p in parts])
        ).astype(BF16)
        pool = []
        far = remote_pool(sub_ref, first_ref, second_ref, spread_ref[0:128], d)
        for j in range(2):
            near = [
                rows(
                    [
                        traces[s * 32 : (s + 1) * 32, (4 * j + c) * 128 : (4 * j + c + 1) * 128]
                        for c in range(4)
                    ]
                )
                for s in range(2)
            ]
            pool.append(lanes(near + [far[j]]))
        hot = gather_hot(partner_ref, kind_ref, parity, d)
        got = dot(rows(pool), hot).astype(BF16)
        stacks = [[], []]
        for s in range(2):
            f = 2 * d + s
            kind = jnp.broadcast_to(kind_ref[f : f + 1, :], (32, ELEMENTS))
            quarter = jnp.broadcast_to(quadrant_ref[f : f + 1, :], (32, ELEMENTS))
            group = jnp.where(kind == 1, quarter + 1, jnp.where(kind == 2, 5, 0))
            wanted = [
                jnp.where(group == t, 1.0, 0.0).astype(BF16) for t in range(6)
            ]
            for j in range(2):
                for b in range(9):
                    q = max(0, b - 5)
                    spot = slice(q * 256 + s * 128, q * 256 + (s + 1) * 128)
                    pieces = [
                        got[j * 128 + c * 32 : j * 128 + (c + 1) * 32, spot] for c in range(4)
                    ]
                    if b < 6:
                        pieces = [p * wanted[b] for p in pieces]
                    stacks[j].append(lanes(pieces))
        high = rows(stacks[0])
        low = rows(stacks[1])
        lifted = dot(visc_ref[d], rows([high, low, high]))
        for c in range(4):
            piece = lifted[:, c * 128 : (c + 1) * 128]
            before = acc_in_ref[1 + c] if d == 0 else acc[c]
            acc[c] = before + piece
    metric = time_step * (1.0 + level_ref[...].astype(F32))
    for c in range(5):
        total = acc_in_ref[0] if c == 0 else acc[c - 1]
        change = section_decay * memory_ref[c] + metric * total[0:125]
        memory_out[c] = change
        state_out[c] = state_ref[c] + section_weight * change


def call(body, outs, operands, scratch=(), scalars=0, cost=None):
    specs = [pl.BlockSpec(memory_space=pltpu.SMEM)] * scalars + [
        pl.BlockSpec(memory_space=pltpu.VMEM)
    ] * (len(operands) - scalars)
    return pl.pallas_call(
        body,
        out_shape=[jax.ShapeDtypeStruct(shape, F32) for shape in outs],
        in_specs=specs,
        out_specs=[pl.BlockSpec(memory_space=pltpu.VMEM)] * len(outs),
        scratch_shapes=[pltpu.VMEM(shape, F32) for shape in scratch],
        compiler_params=pltpu.CompilerParams(vmem_limit_bytes=VMEM_LIMIT),
        name=body.__name__,
        interpret=INTERPRET,
    )(*operands)


INTERPRET = False


def exchange(sub, first, second):
    count = lax.axis_size("curve")
    even_up = [(i, i ^ 1) for i in range(count)]
    odd_up = [(i, (i + 1) % count if i % 2 else (i - 1) % count) for i in range(count)]
    return (
        lax.all_to_all(sub, "sub", split_axis=0, concat_axis=0, tiled=True),
        lax.ppermute(first, "curve", even_up),
        lax.ppermute(second, "curve", odd_up),
    )


def picks(send_sub, send_curve, parity):
    place = np.arange(128)
    sub_rows = jnp.pad(send_sub.reshape(8, 12), ((0, 0), (0, 4))).reshape(1, 128)
    curve_rows = jnp.pad(send_curve.reshape(2, 96), ((0, 0), (0, 32)))
    first = jnp.where(parity == 0, curve_rows[1:2], curve_rows[0:1])
    second = jnp.where(parity == 0, curve_rows[0:1], curve_rows[1:2])
    table = jnp.stack([sub_rows, first, second])
    direction = np.stack([(place % 16) // 4, place // 32, place // 32])
    mask = direction[:, None, :] == np.arange(3)[None, :, None]
    return jnp.where(mask, table, -1)


def local(
    state_now,
    section_memory,
    element_level,
    face_kind,
    face_partner,
    face_quadrant,
    send_sub,
    send_curve,
):
    const = {name: jnp.asarray(value) for name, value in constants().items()}
    parity = (lax.axis_index("curve") % 2).astype(jnp.int32)
    parity_arg = parity.reshape(1)
    level = element_level.reshape(1, ELEMENTS)
    pick = picks(send_sub, send_curve, parity)
    messages = [(128, 128), (96, 128), (96, 128)]
    padded5 = (5, 128, ELEMENTS)
    sent = call(
        pack_kernel, messages, (state_now, pick, const["pack_state"]), scratch=[padded5]
    )
    arrived = exchange(*sent)
    volume, gradients = call(
        volume_kernel,
        [padded5, (12, 128, ELEMENTS)],
        (state_now, const["deriv_all"], const["deriv_sum"], const["signs"]),
        scratch=[padded5, (384, 1280)],
    )
    acc, flux, *sent = call(
        surface_kernel,
        [padded5, (3, 4, 128, ELEMENTS)] + messages,
        (
            parity_arg,
            state_now,
            gradients,
            volume,
            level,
            face_kind,
            face_partner,
            face_quadrant,
            *arrived,
            pick,
            const["own"],
            const["spread"],
            const["quads"],
            const["lift"],
            const["pack_flux"],
        ),
        scratch=[padded5, (320, 640), (160, 1024), (128, 1280), (12, 128, ELEMENTS)],
        scalars=1,
    )
    arrived = exchange(*sent)
    (acc,) = call(
        own_viscous_kernel, [padded5], (flux, acc, face_kind, const["own_visc"])
    )
    state_next, memory_next = call(
        final_kernel,
        [(5, 125, ELEMENTS)] * 2,
        (
            parity_arg,
            state_now,
            section_memory,
            level,
            face_kind,
            face_partner,
            face_quadrant,
            flux,
            acc,
            *arrived,
            const["face_rows"],
            const["spread"],
            const["visc"],
        ),
        scratch=[(4, 128, ELEMENTS)],
        scalars=1,
    )
    return (state_next, memory_next)


def solution(mesh):
    placed = (
        P(None, None, ("curve", "sub")),
        P(None, None, ("curve", "sub")),
        P(("curve", "sub")),
        P(None, ("curve", "sub")),
        P(None, None, ("curve", "sub")),
        P(None, ("curve", "sub")),
        P(("curve", "sub"), None, None),
        P(("curve", "sub"), None, None),
    )
    return jax.shard_map(
        local,
        mesh=mesh,
        in_specs=placed,
        out_specs=(P(None, None, ("curve", "sub")), P(None, None, ("curve", "sub"))),
        check_vma=False,
    )
```

time: 441 us -> 67.7 us (0.15); the launches traced: 433 us -> 67.1 us
  local copies, waits for them, and re-layouts: 243 us -> 3.53 us
  other arithmetic: 100 us -> 1.29 us
  matrix products: 43.2 us -> 0 us
  Pallas kernels: 0 us -> 23 us
  between operations: 7.16 us -> 0.76 us
    gather x51 -> x0, local copies, waits for them, and re-layouts: 129 us -> none  [the longest x12 67.1 us: mortar_states(): plus_parts = jnp.moveaxis(jnp.take(pool, axis_partners, axis=2), 2, 0)]
    dot_general x48 -> x0, matrix products: 43.2 us -> none  [the longest x36 27.8 us: project_faces(): jnp.tensordot(project_table[q], parts[q], axes=([1], [1]), precision=high...]
    unnamed x741 -> x18, local copies, waits for them, and re-layouts: 26.8 us -> 2.65 us
    reshape x26 -> x2, local copies, waits for them, and re-layouts: 24.1 us -> 0.78 us  [the longest x1 0.7 us: picks(): send_sub.reshape(8, 12)]
    pallas_call x0 -> x5, Pallas kernels: none -> 23 us  [call(): pl.pallas_call(body, out_shape=[jax.ShapeDtypeStruct(shape, F32) for shap...]
    unnamed x105 -> x0, other arithmetic: 19 us -> none
    mul x33 -> x0, local copies, waits for them, and re-layouts: 17 us -> none  [the longest x30 16.2 us: split_volume(): 0.5 * (rho_s[i] + rho_s[m]) * (0.5 * (normal_s[i] + normal_s[m]))]
    concatenate x15 -> x0, local copies, waits for them, and re-layouts: 16.3 us -> none  [the longest x9 14.1 us: assemble_pools(): jnp.concatenate([own_lists[d], sub_parts[:, :, :, d, :].reshape(component...]
  transfers between devices with their start and end apart: 6 -> 6, of which waited for: 0 -> 1; matrix products, arithmetic and copies ran while one was open for 21% -> 1% of each run, Pallas kernels for 0% -> 9%
where the time goes in v1:
time: 67.7 us; the launch traced here: 67.1 us
  starting transfers between devices  37.6 us (56%)
  Pallas kernels  23 us (34%)
  local copies, waits for them, and re-layouts  3.53 us (5%)
  other arithmetic  1.29 us (2%)
  waiting for transfers between devices  0.92 us (1%)
  between operations  0.76 us (1%)
    pallas_call x5, Pallas kernels, call(): pl.pallas_call(body, out_shape=[jax.ShapeDtypeStruct(shape, F32) for shap...  23 us
    all_to_all x2, starting transfers between devices, exchange(): lax.all_to_all(sub, 'sub', split_axis=0, concat_axis=0, tiled=True)  19.1 us
    ppermute x2, starting transfers between devices, exchange(): lax.ppermute(second, 'curve', odd_up)  14.7 us
    ppermute x2, starting transfers between devices, exchange(): lax.ppermute(first, 'curve', even_up)  3.82 us
    unnamed x18, local copies, waits for them, and re-layouts  2.65 us
  transfers between devices with their start and end apart: 6, of which 1 were waited for; matrix products, arithmetic and copies ran while one was open for 1% of the time, Pallas kernels for 9%

profile of v1, /device:TPU:1, one launch (start us, length us, event | category | flops | bytes accessed | tf_op | source)
XLA Modules:
  0.0 67.1 jit_solution(2504084103824426098)
XLA Ops:
  0.7 0.7 %copy.27 = s32[2,3,32]{2,1,0:T(4,128)S(1)} copy(s32[2,3,32]{2,0,1:T(2,128)} %param.28) | data formatting | bytes 1536 | tf_op args[7]
  1.3 0.1 reshape.23
  1.4 0.7 %reshape.22 = s32[8,12]{0,1:T(8,128)S(1)} reshape(s32[8,3,4]{0,2,1:T(4,128)} %param.27) | data formatting | bytes 768 | tf_op jit(solution)/shard_map/reshape | solution.py:596
  2.1 0.1 copy.31
  2.2 0.1 stack_reshape.3
  2.3 1.3 %broadcast_select_fusion.pick_ref = s32[3,3,128]{2,1,0:T(4,128)} fusion(pred[3,3,128]{2,1,0:T(4,128)(4,1)} %constant.59.clone, s32[3,128]{1,0:T(4,128)S(1)} %bitcast.19), kind=kLoop, calls=%fused_computation | loop fusion | flops 1152 | bytes 7296 | tf_op jit(solution)/shard_map/jit(_where)/select_n | solution.py:603
  3.6 3.0 %pack_kernel.1 = (f32[128,128]{1,0:T(8,128)}, f32[96,128]{1,0:T(8,128)}, f32[96,128]{1,0:T(8,128)}) custom-call(f32[5,125,128]{2,1,0:T(8,128)} %state_ref.7, s32[3,3,128]{2,1,0:T(4,128)} %broadcast_select_fusion.pick_ref, bf16[3,256,640]{2,1,0:T(8,128)(2,1)} %constant.53.clone.pack_ref), custom_call_target="tpu_custom_call" | custom-call | tf_op jit(solution)/shard_map/pack_kernel/pallas_call | solution.py:568
  6.6 13.8 %all-to-all-start = ((f32[8,16,128]{2,1,0:T(8,128)}), f32[8,16,128]{2,1,0:T(8,128)S(1)}, u32[]{:S(2)}, u32[]{:S(2)}) async-start(f32[8,16,128]{2,1,0:T(8,128)} %bitcast.18), calls=%async_computation | async-start | bytes 131072 | tf_op jit(solution)/shard_map/all_to_all | solution.py:588
  20.3 1.9 %collective-permute-start = (f32[96,128]{1,0:T(8,128)}, f32[96,128]{1,0:T(8,128)S(1)}, u32[]{:S(2)}, u32[]{:S(2)}) collective-permute-start(f32[96,128]{1,0:T(8,128)} %get-tuple-element.15), channel_id=1, source_target_pairs={{0,8},{8,0},{16,24},{24,16},{32,40},{40,32},{48,56},{56,48},{64,72... | collective-permute-start | bytes 147464 | tf_op jit(solution)/shard_map/ppermute | solution.py:589
  22.3 9.5 %collective-permute-start.1 = (f32[96,128]{1,0:T(8,128)}, f32[96,128]{1,0:T(8,128)S(1)}, u32[]{:S(2)}, u32[]{:S(2)}) collective-permute-start(f32[96,128]{1,0:T(8,128)} %get-tuple-element.16), channel_id=1, source_target_pairs={{0,760},{8,16},{16,8},{24,32},{32,24},{40,48},{48,40},{56,64},{64,... | collective-permute-start | bytes 147464 | tf_op jit(solution)/shard_map/ppermute | solution.py:590
  31.8 0.6 copy.29.partner_ref
  32.4 3.4 %volume_kernel.1 = (f32[5,128,128]{2,1,0:T(8,128)}, f32[12,128,128]{2,1,0:T(8,128)}) custom-call(f32[5,125,128]{2,1,0:T(8,128)} %state_ref.7, bf16[384,384]{1,0:T(8,128)(2,1)} %constant.47.clone.all_ref, bf16[128,1152]{1,0:T(8,128)(2,1)} %constant.48.clone.sum_ref, f32[3,128,128]{2,1,0:T(8,128)} %constant.58.clone.sign_ref), custom_call_target="tpu_custom_call" | custom-call | tf_op jit(solution)/shard_map/volume_kernel/pallas_call | solution.py:568
  35.8 0.6 copy-done.2
  36.4 0.0 copy-done.3
  36.4 0.0 copy-done
  36.5 8.6 %surface_kernel.1 = (f32[5,128,128]{2,1,0:T(8,128)}, f32[3,4,128,128]{3,2,1,0:T(8,128)}, f32[128,128]{1,0:T(8,128)}, f32[96,128]{1,0:T(8,128)}, f32[96,128]{1,0:T(8,128)}) custom-call(s32[1]{0:T(128)} %bitcast.parity_ref, f32[5,125,128]{2,1,0:T(8,128)} %state_ref.7, f32[12,128,128]{2,1,0:T(8,128)} %get-tuple-element.12.grad_in_ref, ...), custom_call_target="tpu_custom_call" | custom-call | tf_op jit(solution)/shard_map/surface_kernel/pallas_call | solution.py:568
  45.0 5.4 %all-to-all-start.1 = ((f32[8,16,128]{2,1,0:T(8,128)}), f32[8,16,128]{2,1,0:T(8,128)S(1)}, u32[]{:S(2)}, u32[]{:S(2)}) async-start(f32[8,16,128]{2,1,0:T(8,128)} %bitcast.17), calls=%async_computation.1 | async-start | bytes 131072 | tf_op jit(solution)/shard_map/all_to_all | solution.py:588
  50.4 1.9 %collective-permute-start.2 = (f32[96,128]{1,0:T(8,128)}, f32[96,128]{1,0:T(8,128)S(1)}, u32[]{:S(2)}, u32[]{:S(2)}) collective-permute-start(f32[96,128]{1,0:T(8,128)} %get-tuple-element.20), channel_id=1, source_target_pairs={{0,8},{8,0},{16,24},{24,16},{32,40},{40,32},{48,56},{56,48},{64,72... | collective-permute-start | bytes 147464 | tf_op jit(solution)/shard_map/ppermute | solution.py:589
  52.3 5.2 %collective-permute-start.3 = (f32[96,128]{1,0:T(8,128)}, f32[96,128]{1,0:T(8,128)S(1)}, u32[]{:S(2)}, u32[]{:S(2)}) collective-permute-start(f32[96,128]{1,0:T(8,128)} %get-tuple-element.21), channel_id=1, source_target_pairs={{0,760},{8,16},{16,8},{24,32},{32,24},{40,48},{48,40},{56,64},{64,... | collective-permute-start | bytes 147464 | tf_op jit(solution)/shard_map/ppermute | solution.py:590
  57.5 2.7 %own_viscous_kernel.1.acc_in_ref = f32[5,128,128]{2,1,0:T(8,128)} custom-call(f32[3,4,128,128]{3,2,1,0:T(8,128)} %get-tuple-element.17.flux_ref, f32[5,128,128]{2,1,0:T(8,128)} %get-tuple-element.18.acc_in_ref, s32[6,128]{1,0:T(8,128)} %kind_ref.5, bf16[128,2304]{1,0:T(8,128)(2,1)} %constant.55.clone.matrix_ref), custom_call_target="tpu_custom_call" | custom-call | tf_op jit(solution)/shard_map/own_viscous_kernel/pallas_call | solution.py:568
  60.2 0.9 %collective-permute-done.3.second_ref = f32[96,128]{1,0:T(8,128)S(1)} collective-permute-done((f32[96,128]{1,0:T(8,128)}, f32[96,128]{1,0:T(8,128)S(1)}, u32[]{:S(2)}, u32[]{:S(2)}) %collective-permute-start.3) | collective-permute-done | bytes 49184 | tf_op jit(solution)/shard_map/ppermute | solution.py:590
  61.1 0.6 copy-done.5
  61.7 0.0 copy-done.1
  61.7 5.4 %final_kernel.1 = (f32[5,125,128]{2,1,0:T(8,128)}, f32[5,125,128]{2,1,0:T(8,128)}) custom-call(s32[1]{0:T(128)} %bitcast.parity_ref, f32[5,125,128]{2,1,0:T(8,128)} %state_ref.7, f32[5,125,128]{2,1,0:T(8,128)} %memory_ref.1, s32[1,128]{1,0:T(1,128)} %bitcast.21, s32[6,128]{1,0:T(8,128)} %kind_ref.5, s32[4,6,128]{2,1,0:T(8,128)} %copy.29.partner_ref, ...), custom_call_target="tpu_custom_call" | custom-call | tf_op jit(solution)/shard_map/final_kernel/pallas_call | solution.py:568
  (18 shorter events, 0.1 us)
Async XLA Ops:
  0.6 31.1 %copy-start.6 = (s32[4,6,128]{2,0,1:T(4,128)S(1)}, s32[4,6,128]{2,0,1:T(4,128)}, u32[]{:S(2)}) copy-start(s32[4,6,128]{2,0,1:T(4,128)} %param.25) | copy-start | bytes 36868
  6.6 29.2 %all-to-all-start = ((f32[8,16,128]{2,1,0:T(8,128)}), f32[8,16,128]{2,1,0:T(8,128)S(1)}, u32[]{:S(2)}, u32[]{:S(2)}) async-start(f32[8,16,128]{2,1,0:T(8,128)} %bitcast.18), calls=%async_computation | async-start | bytes 131072 | tf_op jit(solution)/shard_map/all_to_all | solution.py:588
  20.3 15.4 %collective-permute-start = (f32[96,128]{1,0:T(8,128)}, f32[96,128]{1,0:T(8,128)S(1)}, u32[]{:S(2)}, u32[]{:S(2)}) collective-permute-start(f32[96,128]{1,0:T(8,128)} %get-tuple-element.15), channel_id=1, source_target_pairs={{0,8},{8,0},{16,24},{24,16},{32,40},{40,32},{48,56},{56,48},{64,72... | collective-permute-start | bytes 147464 | tf_op jit(solution)/shard_map/ppermute | solution.py:589
  22.3 13.5 %collective-permute-start.1 = (f32[96,128]{1,0:T(8,128)}, f32[96,128]{1,0:T(8,128)S(1)}, u32[]{:S(2)}, u32[]{:S(2)}) collective-permute-start(f32[96,128]{1,0:T(8,128)} %get-tuple-element.16), channel_id=1, source_target_pairs={{0,760},{8,16},{16,8},{24,32},{32,24},{40,48},{48,40},{56,64},{64,... | collective-permute-start | bytes 147464 | tf_op jit(solution)/shard_map/ppermute | solution.py:590
  35.8 0.6 copy-start.2
  35.8 0.6 copy-start.3
  35.8 0.6 copy-start
  45.0 16.1 %all-to-all-start.1 = ((f32[8,16,128]{2,1,0:T(8,128)}), f32[8,16,128]{2,1,0:T(8,128)S(1)}, u32[]{:S(2)}, u32[]{:S(2)}) async-start(f32[8,16,128]{2,1,0:T(8,128)} %bitcast.17), calls=%async_computation.1 | async-start | bytes 131072 | tf_op jit(solution)/shard_map/all_to_all | solution.py:588
  50.4 9.8 %collective-permute-start.2 = (f32[96,128]{1,0:T(8,128)}, f32[96,128]{1,0:T(8,128)S(1)}, u32[]{:S(2)}, u32[]{:S(2)}) collective-permute-start(f32[96,128]{1,0:T(8,128)} %get-tuple-element.20), channel_id=1, source_target_pairs={{0,8},{8,0},{16,24},{24,16},{32,40},{40,32},{48,56},{56,48},{64,72... | collective-permute-start | bytes 147464 | tf_op jit(solution)/shard_map/ppermute | solution.py:589
  52.3 8.8 %collective-permute-start.3 = (f32[96,128]{1,0:T(8,128)}, f32[96,128]{1,0:T(8,128)S(1)}, u32[]{:S(2)}, u32[]{:S(2)}) collective-permute-start(f32[96,128]{1,0:T(8,128)} %get-tuple-element.21), channel_id=1, source_target_pairs={{0,760},{8,16},{16,8},{24,32},{32,24},{40,48},{48,40},{56,64},{64,... | collective-permute-start | bytes 147464 | tf_op jit(solution)/shard_map/ppermute | solution.py:590
  60.2 0.9 %copy-start.4 = (f32[96,128]{1,0:T(8,128)}, f32[96,128]{1,0:T(8,128)S(1)}, u32[]{:S(2)}) copy-start(f32[96,128]{1,0:T(8,128)S(1)} %collective-permute-done.2.first_ref) | copy-start | bytes 147460
  61.1 0.6 copy-start.5
  61.1 0.6 copy-start.1

commit v2 on v1

v2 whole, which is shorter than its diff:
```python
import functools
import math

import jax
import jax.numpy as jnp
import ml_dtypes
import numpy as np
from jax import lax
from jax.experimental import pallas as pl
from jax.experimental.pallas import tpu as pltpu
from jax.sharding import PartitionSpec as P

viscosity = 0.1
conduction = 0.1 * 1.4 / (0.4 * 0.72)
time_step = 0.02
section_decay = -567301805773.0 / 1357537059087.0
section_weight = 5161836677717.0 / 13612068292357.0
EDGE = 0.1
F32, BF16 = jnp.float32, jnp.bfloat16
ELEMENTS = 128
VMEM_LIMIT = 56 * 1024 * 1024


def node_tables():
    nodes = np.array([-1.0, -math.sqrt(3.0 / 7.0), 0.0, math.sqrt(3.0 / 7.0), 1.0])
    weights = np.array([0.1, 49.0 / 90.0, 32.0 / 45.0, 49.0 / 90.0, 0.1])
    prods = np.array(
        [np.prod([nodes[m] - nodes[k] for k in range(5) if k != m]) for m in range(5)]
    )
    deriv = np.zeros((5, 5))
    for i in range(5):
        for m in range(5):
            if i != m:
                deriv[i, m] = prods[i] / prods[m] / (nodes[i] - nodes[m])
        deriv[i, i] = -np.sum(deriv[i])

    def lagrange(points):
        values = np.ones((5, 5))
        for m in range(5):
            for k in range(5):
                if k != m:
                    values[:, m] = values[:, m] * (points - nodes[k]) / (nodes[m] - nodes[k])
        return values

    halves = [lagrange((nodes - 1.0) / 2.0), lagrange((nodes + 1.0) / 2.0)]
    projs = [0.5 * (h * weights[:, None]).T / weights[:, None] for h in halves]
    interp = [np.kron(halves[a], halves[b]) for a in range(2) for b in range(2)]
    project = [np.kron(projs[a], projs[b]) for a in range(2) for b in range(2)]
    return deriv, interp, project


def padded(matrix, rows, cols):
    out = np.zeros((rows, cols))
    out[: matrix.shape[0], : matrix.shape[1]] = matrix
    return out


def split_np(matrix):
    high = matrix.astype(np.float32).astype(ml_dtypes.bfloat16)
    low = (matrix - high.astype(np.float64)).astype(np.float32).astype(ml_dtypes.bfloat16)
    return high, low


def stack3(matrix):
    high, low = split_np(matrix)
    return np.concatenate([high, high, low], axis=1)


def stack2(matrix):
    high, low = split_np(matrix)
    top = np.concatenate([high, high], axis=1)
    return np.concatenate([top, np.concatenate([low, np.zeros_like(low)], axis=1)], axis=0)


@functools.lru_cache(maxsize=None)
def constants():
    deriv, interp, project = node_tables()
    eye5 = np.eye(5)
    big = [
        np.kron(np.kron(eye5, eye5), deriv),
        np.kron(np.kron(eye5, deriv), eye5),
        np.kron(np.kron(deriv, eye5), eye5),
    ]
    index = np.arange(125)
    coord = [index % 5, (index // 5) % 5, index // 25]
    trace = {}
    for d in range(3):
        for s in range(2):
            rows = index[coord[d] == 4 * s]
            t = np.zeros((25, 125))
            t[np.arange(25), rows] = 1.0
            trace[d, s] = t
    sigma = (-1.0, 1.0)
    out = {}
    out["deriv"] = np.stack(
        [np.concatenate(split_np(padded(big[d], 128, 128)), axis=1) for d in range(3)]
    )
    spread = np.zeros((160, 128))
    for c in range(5):
        spread[c * 32 : c * 32 + 25, c * 25 : c * 25 + 25] = np.eye(25)
    out["spread"] = spread.astype(ml_dtypes.bfloat16)
    for comps, name in ((5, "compact_state"), (4, "compact_flux")):
        out[name] = np.tile(spread[: 32 * comps].T, (1, 2)).astype(ml_dtypes.bfloat16)
    out["quads"] = stack3(np.concatenate([padded(interp[q], 32, 32) for q in range(4)], axis=0))
    out["project"] = stack2(np.concatenate([padded(project[q], 32, 32) for q in range(4)], axis=1))
    both = sum(project[q] @ interp[q] for q in range(4))
    mixers = [np.eye(25)] + interp + project + [both - np.eye(25)]
    out["mixers"] = stack2(np.concatenate([padded(m, 32, 32) for m in mixers], axis=1))
    out["faces"] = np.stack(
        [
            np.concatenate([padded(trace[d, s], 32, 128) for s in range(2)], axis=0)
            for d in range(3)
        ]
    ).astype(ml_dtypes.bfloat16)
    for name, signed in (("place_state", False), ("place_flux", True)):
        out[name] = np.stack(
            [
                np.concatenate(
                    [
                        padded((sigma[s] if signed else 1.0) * 5.0 * trace[d, s].T, 128, 32)
                        for s in (0, 1, 0, 1)
                    ],
                    axis=1,
                )
                for d in range(3)
            ]
        ).astype(ml_dtypes.bfloat16)
    return out


def split(x):
    high = x.astype(BF16)
    return high, (x - high.astype(F32)).astype(BF16)


def dot(a, b):
    return lax.dot_general(a, b, (((1,), (0,)), ((), ())), preferred_element_type=F32)


def dot_two(a, high, low):
    both = dot(a, rows([high, low]))
    half = a.shape[0] // 2
    return both[0:half] + both[half:]


def dot_nt(a, b):
    return lax.dot_general(a, b, (((1,), (1,)), ((), ())), preferred_element_type=F32)


def lanes(parts):
    return jnp.concatenate(parts, axis=1)


def rows(parts):
    return jnp.concatenate(parts, axis=0)


def one_hot(index_row, count):
    width = index_row.shape[1]
    numbers = lax.broadcasted_iota(jnp.int32, (count, width), 0)
    return jnp.where(numbers == index_row, 1.0, 0.0).astype(BF16)


def load_padded(ref, pad, count):
    for c in range(count):
        pad[c, 120:128, :] = jnp.full((8, ELEMENTS), 1.0 if c in (0, 4) else 0.0, F32)
        pad[c, 0:125, :] = ref[c]


def point_values(u):
    inverse = 1.0 / u[0]
    vel = [u[1 + k] * inverse for k in range(3)]
    kinetic = u[1] * vel[0] + u[2] * vel[1] + u[3] * vel[2]
    pressure = 0.4 * (u[4] - 0.5 * kinetic)
    return inverse, vel, pressure


def sent_faces(sub_ref, curve_ref):
    place = lax.broadcasted_iota(jnp.int32, (1, 128), 1)
    spot = lax.broadcasted_iota(jnp.int32, (4, 128), 0)
    peer = lax.broadcasted_iota(jnp.int32, (8, 128), 1)
    peers = jnp.where(
        lax.shift_right_logical(peer, 4) == lax.broadcasted_iota(jnp.int32, (8, 128), 0), 1.0, 0.0
    ).astype(BF16)
    slot = lax.broadcasted_iota(jnp.int32, (32, 128), 1)
    slots = jnp.where(
        (slot & 31) == lax.broadcasted_iota(jnp.int32, (32, 128), 0), 1.0, 0.0
    ).astype(BF16)
    sub, lower, upper = [], [], []
    for d in range(3):
        wide = dot(sub_ref[d].astype(F32).astype(BF16), peers)
        wide = jnp.where((place & 3) == spot, wide, 0.0)
        row = jnp.sum(wide, axis=0, keepdims=True).astype(jnp.int32)
        sub.append(jnp.where((lax.shift_right_logical(place, 2) & 3) == d, row, -1))
        wide = dot(curve_ref[d].astype(F32).astype(BF16), slots).astype(jnp.int32)
        here = lax.shift_right_logical(place, 5) == d
        lower.append(jnp.where(here, wide[1:2], -1))
        upper.append(jnp.where(here, wide[0:1], -1))
    return sub, lower, upper


def face_values(faces, parts):
    return dot(faces, lanes([p[0] for p in parts] + [p[1] for p in parts])).astype(BF16)


def pool_rows(traces, count):
    def block(j, c):
        spot = slice((j * count + c) * 128, (j * count + c + 1) * 128)
        return lanes([traces[0:32, spot], traces[32:64, spot]])

    return [rows([block(j, c) for c in range(count)]) for j in range(2)]


def send_pack(traces, count, picks, compact, outs):
    data = lanes([rows(pool_rows(traces[d], count)) for d in range(3)])
    hot = lanes(
        [rows([one_hot(picks[t][d], 256) for d in range(3)]) for t in range(3)]
    )
    found = dot(compact, dot(data, hot).astype(BF16))
    for t in range(3):
        outs[t][...] = jnp.transpose(found[:, t * 128 : (t + 1) * 128])[0 : outs[t].shape[0]]


def pack_kernel(
    state_ref,
    faces_ref,
    pick_sub_ref,
    pick_curve_ref,
    compact_ref,
    sub_ref,
    lower_ref,
    upper_ref,
    pad,
):
    load_padded(state_ref, pad, 5)
    parts = [split(pad[c]) for c in range(5)]
    traces = [face_values(faces_ref[d], parts) for d in range(3)]
    picks = sent_faces(pick_sub_ref, pick_curve_ref)
    send_pack(traces, 5, picks, compact_ref[...], (sub_ref, lower_ref, upper_ref))


def node_places():
    numbers = lax.broadcasted_iota(jnp.int32, (128, ELEMENTS), 0)
    return (numbers % 5, (numbers // 5) % 5, numbers // 25)


def edge_signs():
    return [
        jnp.where(at == 4, 1.0 / EDGE, jnp.where(at == 0, -1.0 / EDGE, 0.0)) for at in node_places()
    ]


def deriv_sum(deriv_ref):
    high = [deriv_ref[d, :, 0:128] for d in range(3)]
    low = [deriv_ref[d, :, 128:256] for d in range(3)]
    none = jnp.zeros((128, 128), BF16)
    top = lanes([x for d in range(3) for x in (high[d], high[d])])
    return rows([top, lanes([x for d in range(3) for x in (low[d], none)])])


def dot_sum(a, parts):
    both = dot(a, rows(parts))
    return both[0:128] + both[128:256]


def volume_part(pad, deriv_ref, vol_ref, grad_ref, res):
    sign_ref = edge_signs()
    summed = deriv_sum(deriv_ref)
    none = jnp.zeros((128, 128), BF16)
    each = [
        rows(
            [
                lanes([deriv_ref[d, :, 0:128], deriv_ref[d, :, 0:128]]),
                lanes([deriv_ref[d, :, 128:256], none]),
            ]
        )
        for d in range(3)
    ]
    u = [pad[c] for c in range(5)]
    inverse, vel, pressure = point_values(u)
    total = u[4] + pressure
    enthalpy = total * inverse
    temperature = pressure * inverse
    fields = [u[0], vel[0], vel[1], vel[2], u[1], u[2], u[3], enthalpy, total, temperature]
    for f in range(0, 10, 2):
        pair = [split(fields[f]), split(fields[f + 1])]
        high, low = (lanes([pair[0][j], pair[1][j]]) for j in range(2))
        for d in range(3):
            res[d * 128 : (d + 1) * 128, f * 128 : (f + 2) * 128] = dot_two(each[d], high, low)

    def der(f, d):
        return res[d * 128 : (d + 1) * 128, f * 128 : (f + 1) * 128]

    for d in range(3):
        for v, f in enumerate((1, 2, 3, 9)):
            grad_ref[3 * v + d] = der(f, d) - sign_ref[d] * fields[f]
    div_vel = der(1, 0) + der(2, 1) + der(3, 2)
    div_mom = der(4, 0) + der(5, 1) + der(6, 2)
    advect = vel[0] * der(0, 0) + vel[1] * der(0, 1) + vel[2] * der(0, 2)
    carry = advect + div_mom
    mass = 0.5 * (u[0] * div_vel + carry)
    edge_mass = sign_ref[0] * u[1] + sign_ref[1] * u[2] + sign_ref[2] * u[3]
    vol_ref[0] = edge_mass - mass
    specific = [vel[0], vel[1], vel[2], enthalpy]
    full = [u[1], u[2], u[3], total]
    for k in range(4):
        cross = []
        direct = []
        edge = None
        for d in range(3):
            product = full[k] * vel[d]
            flux = product + pressure if k == d else product
            edge_d = sign_ref[d] * flux
            edge = edge_d if edge is None else edge + edge_d
            h, l = split(specific[k] * vel[d])
            cross += [h, l]
            h, l = split(product + 4.0 * pressure if k == d else product)
            direct += [h, l]
        both = dot_sum(summed, [lanes(list(p)) for p in zip(cross, direct)])
        f_spec, f_full = (1 + k, 4 + k) if k < 3 else (7, 8)
        quad = full[k] * div_vel + specific[k] * carry + u[0] * both[:, 0:128] + both[:, 128:256]
        for d in range(3):
            quad = quad + u[1 + d] * der(f_spec, d) + vel[d] * der(f_full, d)
        vol_ref[1 + k] = edge - 0.25 * quad


def partner_rows(index, d):
    peer = 256 + lax.shift_right_logical(index - 256, 2) * 16 + (index & 3) + 4 * d
    return jnp.where(index < 256, index, jnp.where(index < 288, peer, index + 96))


def gather_hot(partner_ref, kind_ref, hot, d):
    near = lax.broadcasted_iota(jnp.int32, (256, ELEMENTS), 0)
    far = near[0:192] + 256
    for q in range(4):
        for s in range(2):
            f = 2 * d + s
            row = partner_rows(partner_ref[f, q : q + 1, :], d)
            if q > 0:
                row = jnp.where(kind_ref[f : f + 1, :] == 2, row, -1)
            spot = slice(q * 256 + s * 128, q * 256 + (s + 1) * 128)
            hot[0:256, spot] = jnp.where(near == row, 1.0, 0.0).astype(BF16)
            hot[256:448, spot] = jnp.where(far == row, 1.0, 0.0).astype(BF16)


def remote_pool(sub_ref, lower_ref, upper_ref, spread, d):
    arrived = rows(
        [sub_ref[...], lower_ref[32 * d : 32 * d + 32, :], upper_ref[32 * d : 32 * d + 32, :]]
    )
    h, l = split(arrived)
    return dot_nt(spread, h).astype(BF16), dot_nt(spread, l).astype(BF16)


def surface_kernel(
    sub_ref,
    lower_ref,
    upper_ref,
    state_ref,
    deriv_ref,
    level_ref,
    kind_ref,
    partner_ref,
    quadrant_ref,
    faces_ref,
    spread_ref,
    quads_ref,
    project_ref,
    place_ref,
    pick_sub_ref,
    pick_curve_ref,
    compact_ref,
    acc_ref,
    flux_ref,
    sub_out,
    lower_out,
    upper_out,
    pad,
    res,
    hots,
    owns,
    gots,
    quads,
    grad,
):
    load_padded(state_ref, pad, 5)
    volume_part(pad, deriv_ref, acc_ref, grad, res)
    state_parts = [split(pad[c]) for c in range(5)]
    metric = 1.0 + level_ref[...].astype(F32)
    spare = jnp.where(
        lax.broadcasted_iota(jnp.int32, (32, ELEMENTS), 0) >= 25, 1.0, 0.0
    ).astype(F32)
    for d in range(3):
        own, got, quad, hot = (x.at[d] for x in (owns, gots, quads, hots))
        traces = face_values(faces_ref[d], state_parts)
        own[...] = traces[:, 0:640].astype(F32) + traces[:, 640:1280].astype(F32)
        near = pool_rows(traces, 5)
        gather_hot(partner_ref, kind_ref, hot, d)
        far = remote_pool(sub_ref, lower_ref, upper_ref, spread_ref[...], d)
        pool = rows([lanes([near[j], far[j]]) for j in range(2)])
        both = dot(pool, hot[...])
        got[...] = both[0:160] + both[160:320]
        big = lanes([kind_ref[2 * d + s : 2 * d + s + 1, :] for s in range(2)])
        big = jnp.broadcast_to(big, (32, 2 * ELEMENTS)) == 2
        parts = []
        for c in range(5):
            mine = lanes([own[s * 32 : s * 32 + 32, c * 128 : (c + 1) * 128] for s in range(2)])
            parts.append(split(jnp.where(big, mine, got[c * 32 : (c + 1) * 32, 0:256])))
        first_h = lanes([h for h, l in parts])
        first_l = lanes([l for h, l in parts])
        quad[...] = dot(quads_ref[...], rows([first_h, first_l, first_h]))
        stacks = {0: [], 1: []}
        for s in range(2):
            f = 2 * d + s
            sign = 2 * s - 1
            kind = jnp.broadcast_to(kind_ref[f : f + 1, :], (32, ELEMENTS))
            quarter = jnp.broadcast_to(quadrant_ref[f : f + 1, :], (32, ELEMENTS))
            is_big = kind == 2
            is_small = kind == 1
            for q in range(4):
                left, far = [], []
                for c in range(5):
                    spot = slice(c * 128, (c + 1) * 128)
                    wide = slice(c * 256 + s * 128, c * 256 + (s + 1) * 128)
                    minus = quad[32 * q : 32 * q + 32, wide]
                    plus = got[
                        c * 32 : (c + 1) * 32, q * 256 + s * 128 : q * 256 + (s + 1) * 128
                    ]
                    if q == 0:
                        minus = jnp.where(is_big, minus, own[s * 32 : s * 32 + 32, spot])
                        part = quad[96:128, wide]
                        for t in (2, 1, 0):
                            part = jnp.where(quarter == t, quad[32 * t : 32 * t + 32, wide], part)
                        plus = jnp.where(is_small, part, plus)
                    if c in (0, 4):
                        minus = minus + spare
                        plus = plus + spare
                    left.append(minus)
                    far.append(plus)
                if q > 0:
                    left[0] = jnp.where(is_big, left[0], 1.0)
                    far[0] = jnp.where(is_big, far[0], 1.0)
                inv_l, vel_l, press_l = point_values(left)
                inv_r, vel_r, press_r = point_values(far)
                temp_l, temp_r = press_l * inv_l, press_r * inv_r
                speed = jnp.maximum(
                    jnp.abs(vel_l[d]) + jnp.sqrt(1.4 * temp_l),
                    jnp.abs(vel_r[d]) + jnp.sqrt(1.4 * temp_r),
                )
                values = []
                for c in range(5):
                    if c == 0:
                        central = left[1 + d] + far[1 + d]
                    elif c == 4:
                        central = (left[4] + press_l) * vel_l[d] + (far[4] + press_r) * vel_r[d]
                    else:
                        central = left[c] * vel_l[d] + far[c] * vel_r[d]
                        if c == 1 + d:
                            central = central + (press_l + press_r)
                    jump = speed * (far[c] - left[c])
                    values.append(jump - central if sign > 0 else jump + central)
                for a, b in zip(vel_l + [temp_l], vel_r + [temp_r]):
                    values.append(a + b if sign > 0 else -a - b)
                picked = [split(jnp.where(is_big, v, 0.0)) for v in values]
                stacks[s, q] = [lanes([p[j] for p in picked]) for j in range(2)]
                if q == 0:
                    plain = lanes([jnp.where(is_big, 0.0, v) for v in values])
            stack_h = rows([stacks[s, q][0] for q in range(4)])
            stack_l = rows([stacks[s, q][1] for q in range(4)])
            value = plain + dot_two(project_ref[...], stack_h, stack_l)
            for j, part in enumerate(split(value)):
                stacks[j].append(part)
        lifted = dot(place_ref[d], rows(stacks[0] + stacks[1]))
        for c in range(5):
            acc_ref[c] = acc_ref[c] + lifted[:, c * 128 : (c + 1) * 128]
        for v in range(4):
            grad[3 * v + d] = metric * (
                grad[3 * v + d] + lifted[:, (5 + v) * 128 : (6 + v) * 128]
            )
    acc_ref.send()
    inverse = 1.0 / pad[0]
    vel = [pad[1 + k] * inverse for k in range(3)]
    divergence = (2.0 / 3.0 * viscosity) * (grad[0] + grad[4] + grad[8])
    for d in range(3):
        heat = conduction * grad[9 + d]
        for k in range(3):
            tau = viscosity * (grad[3 * d + k] + grad[3 * k + d])
            if k == d:
                tau = tau - divergence
            flux_ref[d, k] = tau
            heat = heat + vel[k] * tau
        flux_ref[d, 3] = heat
    flux_ref.send()
    traces = [
        face_values(faces_ref[d], [split(flux_ref[d, c]) for c in range(4)]) for d in range(3)
    ]
    picks = sent_faces(pick_sub_ref, pick_curve_ref)
    send_pack(traces, 4, picks, compact_ref[...], (sub_out, lower_out, upper_out))


def own_viscous_part(flux_ref, deriv_ref, acc):
    parts = []
    for d in range(3):
        plain = [split(flux_ref[d, c]) for c in range(4)]
        h = lanes([p[0] for p in plain])
        l = lanes([p[1] for p in plain])
        parts += [h, l]
    both = dot_sum(deriv_sum(deriv_ref), parts)
    half = [0.5 * sign for sign in edge_signs()]
    for c in range(4):
        value = both[:, c * 128 : (c + 1) * 128]
        for d in range(3):
            value = value - half[d] * flux_ref[d, c]
        acc[c] = value


def final_kernel(
    sub_ref,
    lower_ref,
    upper_ref,
    flux_ref,
    deriv_ref,
    faces_ref,
    kind_ref,
    partner_ref,
    spread_ref,
    quadrant_ref,
    mixers_ref,
    place_ref,
    level_ref,
    acc_in_ref,
    memory_ref,
    state_ref,
    state_out,
    memory_out,
    acc,
    hots,
):
    own_viscous_part(flux_ref, deriv_ref, acc)
    for d in range(3):
        hot = hots.at[d]
        traces = face_values(faces_ref[d], [split(flux_ref[d, c]) for c in range(4)])
        near = pool_rows(traces, 4)
        far = remote_pool(sub_ref, lower_ref, upper_ref, spread_ref[0:128, :], d)
        pool = [lanes([near[j], far[j]]) for j in range(2)]
        gather_hot(partner_ref, kind_ref, hot, d)
        got = dot(rows(pool), hot[...]).astype(BF16)
        ends = [[], []]
        for s in range(2):
            f = 2 * d + s
            kind = jnp.broadcast_to(kind_ref[f : f + 1, :], (32, ELEMENTS))
            quarter = jnp.broadcast_to(quadrant_ref[f : f + 1, :], (32, ELEMENTS))
            group = jnp.where(kind == 1, quarter + 1, jnp.where(kind == 2, 5, 0))
            wanted = [jnp.where(group == t, 1.0, 0.0).astype(BF16) for t in range(6)]
            stacks = []
            for j in range(2):
                blocks = []
                for b in range(9):
                    q = max(0, b - 5)
                    spot = slice(q * 256 + s * 128, q * 256 + (s + 1) * 128)
                    pieces = [
                        got[j * 128 + c * 32 : j * 128 + (c + 1) * 32, spot] for c in range(4)
                    ]
                    if b < 6:
                        pieces = [p * wanted[b] for p in pieces]
                    blocks.append(lanes(pieces))
                spot = slice(s * 128, (s + 1) * 128)
                blocks.append(
                    lanes([near[j][c * 32 : (c + 1) * 32, spot] * wanted[5] for c in range(4)])
                )
                stacks.append(rows(blocks))
            value = dot_two(mixers_ref[...], stacks[0], stacks[1])
            for j, part in enumerate(split(value)):
                ends[j].append(part)
        lifted = dot(place_ref[d], rows(ends[0] + ends[1]))
        for c in range(4):
            piece = lifted[:, c * 128 : (c + 1) * 128]
            acc[c] = acc[c] + piece
    metric = time_step * (1.0 + level_ref[...].astype(F32))
    for c in range(5):
        total = acc_in_ref[c] if c == 0 else acc_in_ref[c] + acc[c - 1]
        change = section_decay * memory_ref[c] + metric * total[0:125]
        memory_out[c] = change
        state_out[c] = state_ref[c] + section_weight * change


class Late:
    def __init__(self, near, copy):
        self.near, self.copy = near, copy

    def ready(self):
        if self.copy is not None:
            self.copy.wait()
            self.copy = None
        return self.near

    def __getitem__(self, key):
        return self.ready()[key]


class Early:
    def __init__(self, near, copy):
        self.near, self.copy = near, copy

    def send(self):
        self.copy.start()

    def __getitem__(self, key):
        return self.near[key]

    def __setitem__(self, key, value):
        self.near[key] = value


def placed(arrays):
    if INTERPRET:
        return arrays
    return [pltpu.with_memory_space_constraint(x, pltpu.VMEM) for x in arrays]


def call(body, outs, operands, scratch=(), arrived=(), early=0):
    counts = [len(arrived), len(operands), len(outs), len(operands), early, len(scratch)]

    def kernel(*refs):
        groups, at = [], 0
        for count in counts:
            groups.append(refs[at : at + count])
            at += count
        messages, far, out_refs, near, made, work = groups
        copies = [
            pltpu.make_async_copy(source, target, refs[at].at[i])
            for i, (source, target) in enumerate(zip(far, near))
        ]
        for copy in copies:
            copy.start()
        given = [Late(target, copy) for target, copy in zip(near, copies)]
        whole = [
            Early(source, pltpu.make_async_copy(source, target, refs[at].at[len(far) + i]))
            for i, (source, target) in enumerate(zip(made, out_refs))
        ]
        body(*messages, *given, *whole, *out_refs[early:], *work)
        for late in given:
            late.ready()
        for out in whole:
            out.copy.wait()

    return pl.pallas_call(
        kernel,
        out_shape=[jax.ShapeDtypeStruct(shape, F32) for shape in outs],
        in_specs=[pl.BlockSpec(memory_space=pltpu.VMEM)] * len(arrived)
        + [pl.BlockSpec(memory_space=pl.ANY)] * len(operands),
        out_specs=[pl.BlockSpec(memory_space=pl.ANY)] * early
        + [pl.BlockSpec(memory_space=pltpu.VMEM)] * (len(outs) - early),
        scratch_shapes=[pltpu.VMEM(x.shape, x.dtype) for x in operands]
        + [pltpu.VMEM(shape, F32) for shape in outs[:early]]
        + [pltpu.VMEM(*(o if isinstance(o[0], tuple) else (o, F32))) for o in scratch]
        + [pltpu.SemaphoreType.DMA((len(operands) + early,))],
        compiler_params=pltpu.CompilerParams(vmem_limit_bytes=VMEM_LIMIT),
        name=body.__name__,
        interpret=INTERPRET,
    )(*placed(arrived), *operands)


INTERPRET = False


def exchange(sub, lower, upper):
    count = lax.axis_size("curve")
    return (
        lax.all_to_all(sub, "sub", split_axis=0, concat_axis=0, tiled=True),
        lax.ppermute(lower, "curve", [(i, (i + 1) % count) for i in range(count)]),
        lax.ppermute(upper, "curve", [((i + 1) % count, i) for i in range(count)]),
    )


def local(
    state_now,
    section_memory,
    element_level,
    face_kind,
    face_partner,
    face_quadrant,
    send_sub,
    send_curve,
):
    const = {name: jnp.asarray(value) for name, value in constants().items()}
    level = element_level.reshape(1, ELEMENTS)
    picks = (send_sub.transpose(1, 2, 0), send_curve.transpose(1, 0, 2))
    face_partner = face_partner.transpose(1, 0, 2)
    messages = [(128, 128), (96, 128), (96, 128)]
    padded5 = (5, 128, ELEMENTS)
    hot = ((3, 448, 8 * ELEMENTS), BF16)
    sent = call(
        pack_kernel,
        messages,
        (state_now, const["faces"], *picks, const["compact_state"]),
        scratch=[padded5],
    )
    acc, flux, *sent = call(
        surface_kernel,
        [padded5, (3, 4, 128, ELEMENTS)] + messages,
        (
            state_now,
            const["deriv"],
            level,
            face_kind,
            face_partner,
            face_quadrant,
            const["faces"],
            const["spread"],
            const["quads"],
            const["project"],
            const["place_state"],
            *picks,
            const["compact_flux"],
        ),
        scratch=[
            padded5,
            (384, 1280),
            hot,
            (3, 64, 640),
            (3, 160, 1024),
            (3, 128, 1280),
            (12, 128, ELEMENTS),
        ],
        arrived=exchange(*sent),
        early=2,
    )
    state_next, memory_next = call(
        final_kernel,
        [(5, 125, ELEMENTS)] * 2,
        (
            flux,
            const["deriv"],
            const["faces"],
            face_kind,
            face_partner,
            const["spread"],
            face_quadrant,
            const["mixers"],
            const["place_flux"],
            level,
            acc,
            section_memory,
            state_now,
        ),
        scratch=[(4, 128, ELEMENTS), hot],
        arrived=exchange(*sent),
    )
    return (state_next, memory_next)


def solution(mesh):
    placed = (
        P(None, None, ("curve", "sub")),
        P(None, None, ("curve", "sub")),
        P(("curve", "sub")),
        P(None, ("curve", "sub")),
        P(None, None, ("curve", "sub")),
        P(None, ("curve", "sub")),
        P(("curve", "sub"), None, None),
        P(("curve", "sub"), None, None),
    )
    return jax.shard_map(
        local,
        mesh=mesh,
        in_specs=placed,
        out_specs=(P(None, None, ("curve", "sub")), P(None, None, ("curve", "sub"))),
        check_vma=False,
    )
```

time: 67.7 us -> 62.4 us (0.922)
  Pallas kernels: 23 us -> 18.8 us
  local copies, waits for them, and re-layouts: 3.53 us -> 0.02 us
  starting transfers between devices: 37.6 us -> 40.1 us
  waiting for transfers between devices: 0.92 us -> 2.32 us
  other arithmetic: 1.29 us -> 0 us
    pallas_call x5 -> x3, Pallas kernels: 23 us -> 18.8 us  [call(): pl.pallas_call(kernel, out_shape=[jax.ShapeDtypeStruct(shape, F32) for sh...]
    unnamed x18 -> x8, local copies, waits for them, and re-layouts: 2.65 us -> 0.02 us
    ppermute x4, starting transfers between devices: 18.5 us -> 20.4 us  [the longest x2 16.5 us: exchange(): lax.ppermute(upper, 'curve', [((i + 1) % count, i) for i in range(count)])]
    ppermute x4, waiting for transfers between devices: 0.92 us -> 2.31 us  [the longest x2 2.02 us: exchange(): lax.ppermute(upper, 'curve', [((i + 1) % count, i) for i in range(count)])]
    select_n x1 -> x0, other arithmetic: 1.28 us -> none  [picks(): return jnp.where(mask, table, -1)]
    reshape x2 -> x0, local copies, waits for them, and re-layouts: 0.78 us -> none  [the longest x1 0.7 us: picks(): send_sub.reshape(8, 12)]
  transfers between devices with their start and end apart: 6 -> 6, of which waited for: 1 -> 4; matrix products, arithmetic and copies ran while one was open for 1% -> 0% of each run, Pallas kernels for 9% -> 0%
where the time goes in v2:
time: 62.4 us; the launch traced here: 61.9 us
  starting transfers between devices  40.1 us (64%)
  Pallas kernels  18.8 us (30%)
  waiting for transfers between devices  2.32 us (4%)
  between operations  0.73 us (1%)
    all_to_all x2, starting transfers between devices, exchange(): lax.all_to_all(sub, 'sub', split_axis=0, concat_axis=0, tiled=True)  19.7 us
    pallas_call x3, Pallas kernels, call(): pl.pallas_call(kernel, out_shape=[jax.ShapeDtypeStruct(shape, F32) for sh...  18.8 us
    ppermute x2, starting transfers between devices, exchange(): lax.ppermute(upper, 'curve', [((i + 1) % count, i) for i in range(count)])  16.5 us
    ppermute x2, starting transfers between devices, exchange(): lax.ppermute(lower, 'curve', [(i, (i + 1) % count) for i in range(count)])  3.82 us
    ppermute x2, waiting for transfers between devices, exchange(): lax.ppermute(upper, 'curve', [((i + 1) % count, i) for i in range(count)])  2.02 us
  transfers between devices with their start and end apart: 6, of which 4 were waited for; matrix products, arithmetic and copies ran while one was open for 0% of the time, Pallas kernels for 0%

profile of v2, /device:TPU:1, one launch (start us, length us, event | category | flops | bytes accessed | tf_op | source)
XLA Modules:
  0.0 61.9 jit_solution(11618376936390050240)
XLA Ops:
  0.6 2.9 %pack_kernel.1 = (f32[128,128]{1,0:T(8,128)}, f32[96,128]{1,0:T(8,128)}, f32[96,128]{1,0:T(8,128)}) custom-call(f32[5,125,128]{2,1,0:T(8,128)} %refs_15_.1, bf16[3,64,128]{2,1,0:T(8,128)(2,1)} %constant.27.clone.refs_1_.refs_9_.refs_5_, s32[3,4,8]{2,1,0:T(4,128)} %bitcast.14, s32[3,2,32]{2,1,0:T(2,128)} %bitcast.16, bf16[128,320]{1,0:T(8,128)(2,1)} %constant.22.clone.refs_4_), custom_call_target="tpu_custom_call" | custom-call | tf_op jit(solution)/shard_map/pack_kernel/pallas_call | solution.py:646
  3.6 0.0 copy-start.3
  3.6 0.0 copy-start.2
  3.6 13.9 %all-to-all-start = ((f32[8,16,128]{2,1,0:T(8,128)}), f32[8,16,128]{2,1,0:T(8,128)S(1)}, u32[]{:S(2)}, u32[]{:S(2)}) async-start(f32[8,16,128]{2,1,0:T(8,128)} %bitcast.11), calls=%async_computation | async-start | bytes 131072 | tf_op jit(solution)/shard_map/all_to_all | solution.py:669
  17.5 0.0 copy-done.3
  17.5 1.9 %collective-permute-start = (f32[96,128]{1,0:T(8,128)S(1)}, f32[96,128]{1,0:T(8,128)S(1)}, u32[]{:S(2)}, u32[]{:S(2)}) collective-permute-start(f32[96,128]{1,0:T(8,128)S(1)} %copy-done.3), channel_id=1, source_target_pairs={{0,8},{8,16},{16,24},{24,32},{32,40},{40,48},{48,56},{56,64},{64,7... | collective-permute-start | bytes 147464 | tf_op jit(solution)/shard_map/ppermute | solution.py:670
  19.4 0.0 copy-done.2
  19.4 9.2 %collective-permute-start.1 = (f32[96,128]{1,0:T(8,128)S(1)}, f32[96,128]{1,0:T(8,128)S(1)}, u32[]{:S(2)}, u32[]{:S(2)}) collective-permute-start(f32[96,128]{1,0:T(8,128)S(1)} %copy-done.2), channel_id=1, source_target_pairs={{8,0},{16,8},{24,16},{32,24},{40,32},{48,40},{56,48},{64,56},{72,6... | collective-permute-start | bytes 147464 | tf_op jit(solution)/shard_map/ppermute | solution.py:671
  28.7 0.1 collective-permute-done.refs_1_
  28.8 1.0 %collective-permute-done.1.refs_2_ = f32[96,128]{1,0:T(8,128)S(1)} collective-permute-done((f32[96,128]{1,0:T(8,128)S(1)}, f32[96,128]{1,0:T(8,128)S(1)}, u32[]{:S(2)}, u32[]{:S(2)}) %collective-permute-start.1) | collective-permute-done | bytes 49184 | tf_op jit(solution)/shard_map/ppermute | solution.py:671
  29.9 0.0 all-to-all-done
  29.9 9.9 %surface_kernel.1 = (f32[5,128,128]{2,1,0:T(8,128)}, f32[3,4,128,128]{3,2,1,0:T(8,128)}, f32[128,128]{1,0:T(8,128)}, f32[96,128]{1,0:T(8,128)}, f32[96,128]{1,0:T(8,128)}) custom-call(f32[128,128]{1,0:T(8,128)S(1)} %bitcast.8, f32[96,128]{1,0:T(8,128)S(1)} %collective-permute-done.refs_1_, f32[96,128]{1,0:T(8,128)S(1)} %collective-permute-done.1.refs_2_, ...), custom_call_target="tpu_custom_call" | custom-call | tf_op jit(solution)/shard_map/surface_kernel/pallas_call | solution.py:646
  39.7 0.0 copy-start.1
  39.8 0.0 copy-start
  39.8 5.8 %all-to-all-start.1 = ((f32[8,16,128]{2,1,0:T(8,128)}), f32[8,16,128]{2,1,0:T(8,128)S(1)}, u32[]{:S(2)}, u32[]{:S(2)}) async-start(f32[8,16,128]{2,1,0:T(8,128)} %bitcast.10), calls=%async_computation.1 | async-start | bytes 131072 | tf_op jit(solution)/shard_map/all_to_all | solution.py:669
  45.6 0.0 copy-done.1
  45.6 1.9 %collective-permute-start.2 = (f32[96,128]{1,0:T(8,128)S(1)}, f32[96,128]{1,0:T(8,128)S(1)}, u32[]{:S(2)}, u32[]{:S(2)}) collective-permute-start(f32[96,128]{1,0:T(8,128)S(1)} %copy-done.1), channel_id=1, source_target_pairs={{0,8},{8,16},{16,24},{24,32},{32,40},{40,48},{48,56},{56,64},{64,7... | collective-permute-start | bytes 147464 | tf_op jit(solution)/shard_map/ppermute | solution.py:670
  47.5 0.0 copy-done
  47.5 7.3 %collective-permute-start.3 = (f32[96,128]{1,0:T(8,128)S(1)}, f32[96,128]{1,0:T(8,128)S(1)}, u32[]{:S(2)}, u32[]{:S(2)}) collective-permute-start(f32[96,128]{1,0:T(8,128)S(1)} %copy-done), channel_id=1, source_target_pairs={{8,0},{16,8},{24,16},{32,24},{40,32},{48,40},{56,48},{64,56},{72,6... | collective-permute-start | bytes 147464 | tf_op jit(solution)/shard_map/ppermute | solution.py:671
  54.8 0.1 collective-permute-done.2.refs_1_
  54.9 1.0 %collective-permute-done.3.refs_2_ = f32[96,128]{1,0:T(8,128)S(1)} collective-permute-done((f32[96,128]{1,0:T(8,128)S(1)}, f32[96,128]{1,0:T(8,128)S(1)}, u32[]{:S(2)}, u32[]{:S(2)}) %collective-permute-start.3) | collective-permute-done | bytes 49184 | tf_op jit(solution)/shard_map/ppermute | solution.py:671
  55.9 0.0 all-to-all-done.1
  55.9 5.9 %final_kernel.1 = (f32[5,125,128]{2,1,0:T(8,128)}, f32[5,125,128]{2,1,0:T(8,128)}) custom-call(f32[128,128]{1,0:T(8,128)S(1)} %bitcast.9, f32[96,128]{1,0:T(8,128)S(1)} %collective-permute-done.2.refs_1_, f32[96,128]{1,0:T(8,128)S(1)} %collective-permute-done.3.refs_2_, f32[3,4,128,128]{3,2,1,0:T(8,128)} %get-tuple-element.16.refs_3_, ...), custom_call_target="tpu_custom_call" | custom-call | tf_op jit(solution)/shard_map/final_kernel/pallas_call | solution.py:646
Async XLA Ops:
  3.6 13.9 %copy-start.3 = (f32[96,128]{1,0:T(8,128)S(1)}, f32[96,128]{1,0:T(8,128)}, u32[]{:S(2)}) copy-start(f32[96,128]{1,0:T(8,128)} %get-tuple-element.11) | copy-start | bytes 147460
  3.6 15.8 %copy-start.2 = (f32[96,128]{1,0:T(8,128)S(1)}, f32[96,128]{1,0:T(8,128)}, u32[]{:S(2)}) copy-start(f32[96,128]{1,0:T(8,128)} %get-tuple-element.12) | copy-start | bytes 147460
  3.6 26.3 %all-to-all-start = ((f32[8,16,128]{2,1,0:T(8,128)}), f32[8,16,128]{2,1,0:T(8,128)S(1)}, u32[]{:S(2)}, u32[]{:S(2)}) async-start(f32[8,16,128]{2,1,0:T(8,128)} %bitcast.11), calls=%async_computation | async-start | bytes 131072 | tf_op jit(solution)/shard_map/all_to_all | solution.py:669
  17.5 11.3 %collective-permute-start = (f32[96,128]{1,0:T(8,128)S(1)}, f32[96,128]{1,0:T(8,128)S(1)}, u32[]{:S(2)}, u32[]{:S(2)}) collective-permute-start(f32[96,128]{1,0:T(8,128)S(1)} %copy-done.3), channel_id=1, source_target_pairs={{0,8},{8,16},{16,24},{24,32},{32,40},{40,48},{48,56},{56,64},{64,7... | collective-permute-start | bytes 147464 | tf_op jit(solution)/shard_map/ppermute | solution.py:670
  19.4 10.4 %collective-permute-start.1 = (f32[96,128]{1,0:T(8,128)S(1)}, f32[96,128]{1,0:T(8,128)S(1)}, u32[]{:S(2)}, u32[]{:S(2)}) collective-permute-start(f32[96,128]{1,0:T(8,128)S(1)} %copy-done.2), channel_id=1, source_target_pairs={{8,0},{16,8},{24,16},{32,24},{40,32},{48,40},{56,48},{64,56},{72,6... | collective-permute-start | bytes 147464 | tf_op jit(solution)/shard_map/ppermute | solution.py:671
  39.7 5.8 %copy-start.1 = (f32[96,128]{1,0:T(8,128)S(1)}, f32[96,128]{1,0:T(8,128)}, u32[]{:S(2)}) copy-start(f32[96,128]{1,0:T(8,128)} %get-tuple-element.14) | copy-start | bytes 147460
  39.8 7.7 %copy-start = (f32[96,128]{1,0:T(8,128)S(1)}, f32[96,128]{1,0:T(8,128)}, u32[]{:S(2)}) copy-start(f32[96,128]{1,0:T(8,128)} %get-tuple-element.15) | copy-start | bytes 147460
  39.8 16.2 %all-to-all-start.1 = ((f32[8,16,128]{2,1,0:T(8,128)}), f32[8,16,128]{2,1,0:T(8,128)S(1)}, u32[]{:S(2)}, u32[]{:S(2)}) async-start(f32[8,16,128]{2,1,0:T(8,128)} %bitcast.10), calls=%async_computation.1 | async-start | bytes 131072 | tf_op jit(solution)/shard_map/all_to_all | solution.py:669
  45.6 9.4 %collective-permute-start.2 = (f32[96,128]{1,0:T(8,128)S(1)}, f32[96,128]{1,0:T(8,128)S(1)}, u32[]{:S(2)}, u32[]{:S(2)}) collective-permute-start(f32[96,128]{1,0:T(8,128)S(1)} %copy-done.1), channel_id=1, source_target_pairs={{0,8},{8,16},{16,24},{24,32},{32,40},{40,48},{48,56},{56,64},{64,7... | collective-permute-start | bytes 147464 | tf_op jit(solution)/shard_map/ppermute | solution.py:670
  47.5 8.5 %collective-permute-start.3 = (f32[96,128]{1,0:T(8,128)S(1)}, f32[96,128]{1,0:T(8,128)S(1)}, u32[]{:S(2)}, u32[]{:S(2)}) collective-permute-start(f32[96,128]{1,0:T(8,128)S(1)} %copy-done), channel_id=1, source_target_pairs={{8,0},{16,8},{24,16},{32,24},{40,32},{48,40},{56,48},{64,56},{72,6... | collective-permute-start | bytes 147464 | tf_op jit(solution)/shard_map/ppermute | solution.py:671

commit v3 on v2

--- a/solution.py
+++ b/solution.py
@@ -211,32 +211,34 @@
     return [rows([block(j, c) for c in range(count)]) for j in range(2)]
 
 
-def send_pack(traces, count, picks, compact, outs):
+def send_hot(sub_ref, curve_ref):
+    picks = sent_faces(sub_ref, curve_ref)
+    return lanes([rows([one_hot(picks[t][d], 256) for d in range(3)]) for t in range(3)])
+
+
+def send_pack(traces, count, hot, compact, outs):
     data = lanes([rows(pool_rows(traces[d], count)) for d in range(3)])
-    hot = lanes(
-        [rows([one_hot(picks[t][d], 256) for d in range(3)]) for t in range(3)]
-    )
     found = dot(compact, dot(data, hot).astype(BF16))
     for t in range(3):
         outs[t][...] = jnp.transpose(found[:, t * 128 : (t + 1) * 128])[0 : outs[t].shape[0]]
 
 
 def pack_kernel(
+    pick_sub_ref,
+    pick_curve_ref,
     state_ref,
     faces_ref,
-    pick_sub_ref,
-    pick_curve_ref,
     compact_ref,
     sub_ref,
     lower_ref,
     upper_ref,
     pad,
 ):
+    hot = send_hot(pick_sub_ref, pick_curve_ref)
     load_padded(state_ref, pad, 5)
     parts = [split(pad[c]) for c in range(5)]
     traces = [face_values(faces_ref[d], parts) for d in range(3)]
-    picks = sent_faces(pick_sub_ref, pick_curve_ref)
-    send_pack(traces, 5, picks, compact_ref[...], (sub_ref, lower_ref, upper_ref))
+    send_pack(traces, 5, hot, compact_ref[...], (sub_ref, lower_ref, upper_ref))
 
 
 def node_places():
@@ -294,6 +296,7 @@
     for d in range(3):
         for v, f in enumerate((1, 2, 3, 9)):
             grad_ref[3 * v + d] = der(f, d) - sign_ref[d] * fields[f]
+            grad_ref.send(3 * v + d)
     div_vel = der(1, 0) + der(2, 1) + der(3, 2)
     div_mom = der(4, 0) + der(5, 1) + der(6, 2)
     advect = vel[0] * der(0, 0) + vel[1] * der(0, 1) + vel[2] * der(0, 2)
@@ -301,6 +304,7 @@
     mass = 0.5 * (u[0] * div_vel + carry)
     edge_mass = sign_ref[0] * u[1] + sign_ref[1] * u[2] + sign_ref[2] * u[3]
     vol_ref[0] = edge_mass - mass
+    vol_ref.send(0)
     specific = [vel[0], vel[1], vel[2], enthalpy]
     full = [u[1], u[2], u[3], total]
     for k in range(4):
@@ -322,6 +326,12 @@
         for d in range(3):
             quad = quad + u[1 + d] * der(f_spec, d) + vel[d] * der(f_full, d)
         vol_ref[1 + k] = edge - 0.25 * quad
+        vol_ref.send(1 + k)
+
+
+def volume_kernel(state_ref, deriv_ref, vol_ref, grad_ref, pad, res):
+    load_padded(state_ref, pad, 5)
+    volume_part(pad, deriv_ref, vol_ref, grad_ref, res)
 
 
 def partner_rows(index, d):
@@ -355,17 +365,18 @@
     sub_ref,
     lower_ref,
     upper_ref,
-    state_ref,
-    deriv_ref,
-    level_ref,
     kind_ref,
     partner_ref,
-    quadrant_ref,
+    state_ref,
     faces_ref,
     spread_ref,
     quads_ref,
+    quadrant_ref,
     project_ref,
     place_ref,
+    level_ref,
+    vol_ref,
+    grad_in_ref,
     pick_sub_ref,
     pick_curve_ref,
     compact_ref,
@@ -375,15 +386,15 @@
     lower_out,
     upper_out,
     pad,
-    res,
     hots,
     owns,
     gots,
     quads,
     grad,
 ):
+    for d in range(3):
+        gather_hot(partner_ref, kind_ref, hots.at[d], d)
     load_padded(state_ref, pad, 5)
-    volume_part(pad, deriv_ref, acc_ref, grad, res)
     state_parts = [split(pad[c]) for c in range(5)]
     metric = 1.0 + level_ref[...].astype(F32)
     spare = jnp.where(
@@ -394,7 +405,6 @@
         traces = face_values(faces_ref[d], state_parts)
         own[...] = traces[:, 0:640].astype(F32) + traces[:, 640:1280].astype(F32)
         near = pool_rows(traces, 5)
-        gather_hot(partner_ref, kind_ref, hot, d)
         far = remote_pool(sub_ref, lower_ref, upper_ref, spread_ref[...], d)
         pool = rows([lanes([near[j], far[j]]) for j in range(2)])
         both = dot(pool, hot[...])
@@ -471,12 +481,14 @@
                 stacks[j].append(part)
         lifted = dot(place_ref[d], rows(stacks[0] + stacks[1]))
         for c in range(5):
-            acc_ref[c] = acc_ref[c] + lifted[:, c * 128 : (c + 1) * 128]
+            before = vol_ref[c] if d == 0 else acc_ref[c]
+            acc_ref[c] = before + lifted[:, c * 128 : (c + 1) * 128]
+            if d == 2:
+                acc_ref.send(c)
         for v in range(4):
             grad[3 * v + d] = metric * (
-                grad[3 * v + d] + lifted[:, (5 + v) * 128 : (6 + v) * 128]
+                grad_in_ref[3 * v + d] + lifted[:, (5 + v) * 128 : (6 + v) * 128]
             )
-    acc_ref.send()
     inverse = 1.0 / pad[0]
     vel = [pad[1 + k] * inverse for k in range(3)]
     divergence = (2.0 / 3.0 * viscosity) * (grad[0] + grad[4] + grad[8])
@@ -489,12 +501,12 @@
             flux_ref[d, k] = tau
             heat = heat + vel[k] * tau
         flux_ref[d, 3] = heat
-    flux_ref.send()
+        flux_ref.send(d)
     traces = [
         face_values(faces_ref[d], [split(flux_ref[d, c]) for c in range(4)]) for d in range(3)
     ]
-    picks = sent_faces(pick_sub_ref, pick_curve_ref)
-    send_pack(traces, 4, picks, compact_ref[...], (sub_out, lower_out, upper_out))
+    hot = send_hot(pick_sub_ref, pick_curve_ref)
+    send_pack(traces, 4, hot, compact_ref[...], (sub_out, lower_out, upper_out))
 
 
 def own_viscous_part(flux_ref, deriv_ref, acc):
@@ -517,11 +529,11 @@
     sub_ref,
     lower_ref,
     upper_ref,
+    kind_ref,
+    partner_ref,
     flux_ref,
     deriv_ref,
     faces_ref,
-    kind_ref,
-    partner_ref,
     spread_ref,
     quadrant_ref,
     mixers_ref,
@@ -535,6 +547,8 @@
     acc,
     hots,
 ):
+    for d in range(3):
+        gather_hot(partner_ref, kind_ref, hots.at[d], d)
     own_viscous_part(flux_ref, deriv_ref, acc)
     for d in range(3):
         hot = hots.at[d]
@@ -542,7 +556,6 @@
         near = pool_rows(traces, 4)
         far = remote_pool(sub_ref, lower_ref, upper_ref, spread_ref[0:128, :], d)
         pool = [lanes([near[j], far[j]]) for j in range(2)]
-        gather_hot(partner_ref, kind_ref, hot, d)
         got = dot(rows(pool), hot[...]).astype(BF16)
         ends = [[], []]
         for s in range(2):
@@ -580,7 +593,9 @@
         total = acc_in_ref[c] if c == 0 else acc_in_ref[c] + acc[c - 1]
         change = section_decay * memory_ref[c] + metric * total[0:125]
         memory_out[c] = change
+        memory_out.send(c)
         state_out[c] = state_ref[c] + section_weight * change
+        state_out.send(c)
 
 
 class Late:
@@ -598,11 +613,11 @@
 
 
 class Early:
-    def __init__(self, near, copy):
-        self.near, self.copy = near, copy
-
-    def send(self):
-        self.copy.start()
+    def __init__(self, near, copies):
+        self.near, self.copies = near, copies
+
+    def send(self, i):
+        self.copies[i].start()
 
     def __getitem__(self, key):
         return self.near[key]
@@ -633,15 +648,25 @@
         for copy in copies:
             copy.start()
         given = [Late(target, copy) for target, copy in zip(near, copies)]
-        whole = [
-            Early(source, pltpu.make_async_copy(source, target, refs[at].at[len(far) + i]))
-            for i, (source, target) in enumerate(zip(made, out_refs))
-        ]
+        whole, used = [], len(far)
+        for source, target in zip(made, out_refs):
+            count = source.shape[0]
+            whole.append(
+                Early(
+                    source,
+                    [
+                        pltpu.make_async_copy(source.at[i], target.at[i], refs[at].at[used + i])
+                        for i in range(count)
+                    ],
+                )
+            )
+            used += count
         body(*messages, *given, *whole, *out_refs[early:], *work)
         for late in given:
             late.ready()
         for out in whole:
-            out.copy.wait()
+            for copy in out.copies:
+                copy.wait()
 
     return pl.pallas_call(
         kernel,
@@ -653,7 +678,7 @@
         scratch_shapes=[pltpu.VMEM(x.shape, x.dtype) for x in operands]
         + [pltpu.VMEM(shape, F32) for shape in outs[:early]]
         + [pltpu.VMEM(*(o if isinstance(o[0], tuple) else (o, F32))) for o in scratch]
-        + [pltpu.SemaphoreType.DMA((len(operands) + early,))],
+        + [pltpu.SemaphoreType.DMA((len(operands) + sum(shape[0] for shape in outs[:early]),))],
         compiler_params=pltpu.CompilerParams(vmem_limit_bytes=VMEM_LIMIT),
         name=body.__name__,
         interpret=INTERPRET,
@@ -692,48 +717,56 @@
     sent = call(
         pack_kernel,
         messages,
-        (state_now, const["faces"], *picks, const["compact_state"]),
+        (*picks, state_now, const["faces"], const["compact_state"]),
         scratch=[padded5],
+    )
+    arrived = exchange(*sent)
+    volume, gradients = call(
+        volume_kernel,
+        [padded5, (12, 128, ELEMENTS)],
+        (state_now, const["deriv"]),
+        scratch=[padded5, (384, 1280)],
+        early=2,
     )
     acc, flux, *sent = call(
         surface_kernel,
         [padded5, (3, 4, 128, ELEMENTS)] + messages,
         (
-            state_now,
-            const["deriv"],
-            level,
             face_kind,
             face_partner,
-            face_quadrant,
+            state_now,
             const["faces"],
             const["spread"],
             const["quads"],
+            face_quadrant,
             const["project"],
             const["place_state"],
+            level,
+            volume,
+            gradients,
             *picks,
             const["compact_flux"],
         ),
         scratch=[
             padded5,
-            (384, 1280),
             hot,
             (3, 64, 640),
             (3, 160, 1024),
             (3, 128, 1280),
             (12, 128, ELEMENTS),
         ],
-        arrived=exchange(*sent),
+        arrived=arrived,
         early=2,
     )
     state_next, memory_next = call(
         final_kernel,
         [(5, 125, ELEMENTS)] * 2,
         (
+            face_kind,
+            face_partner,
             flux,
             const["deriv"],
             const["faces"],
-            face_kind,
-            face_partner,
             const["spread"],
             face_quadrant,
             const["mixers"],
@@ -745,6 +778,7 @@
         ),
         scratch=[(4, 128, ELEMENTS), hot],
         arrived=exchange(*sent),
+        early=2,
     )
     return (state_next, memory_next)
 

time: 62.4 us -> 62.6 us (level)
  Pallas kernels: 18.8 us -> 21 us
  waiting for transfers between devices: 2.32 us -> 0.98 us
  starting transfers between devices: 40.1 us -> 39.1 us
    pallas_call x3 -> x4, Pallas kernels: 18.8 us -> 21 us  [call(): pl.pallas_call(kernel, out_shape=[jax.ShapeDtypeStruct(shape, F32) for sh...]
    ppermute x2, waiting for transfers between devices: 2.02 us -> 0.97 us  [exchange(): lax.ppermute(upper, 'curve', [((i + 1) % count, i) for i in range(count)])]
  transfers between devices with their start and end apart: 6 -> 6, of which waited for: 4 -> 1; matrix products, arithmetic and copies ran while one was open for 0% -> 0% of each run, Pallas kernels for 0% -> 5%
where the time goes in v3:
time: 62.6 us; the launch traced here: 61.9 us
  starting transfers between devices  39.1 us (62%)
  Pallas kernels  21 us (34%)
  waiting for transfers between devices  0.98 us (2%)
  between operations  0.93 us (1%)
    pallas_call x4, Pallas kernels, call(): pl.pallas_call(kernel, out_shape=[jax.ShapeDtypeStruct(shape, F32) for sh...  21 us
    all_to_all x2, starting transfers between devices, exchange(): lax.all_to_all(sub, 'sub', split_axis=0, concat_axis=0, tiled=True)  19.1 us
    ppermute x2, starting transfers between devices, exchange(): lax.ppermute(upper, 'curve', [((i + 1) % count, i) for i in range(count)])  16.1 us
    ppermute x2, starting transfers between devices, exchange(): lax.ppermute(lower, 'curve', [(i, (i + 1) % count) for i in range(count)])  3.82 us
  transfers between devices with their start and end apart: 6, of which 1 were waited for; matrix products, arithmetic and copies ran while one was open for 0% of the time, Pallas kernels for 5%

profile of v3, /device:TPU:1, one launch (start us, length us, event | category | flops | bytes accessed | tf_op | source)
XLA Modules:
  0.0 61.9 jit_solution(10132838628005552489)
XLA Ops:
  0.6 2.8 %pack_kernel.1 = (f32[128,128]{1,0:T(8,128)}, f32[96,128]{1,0:T(8,128)}, f32[96,128]{1,0:T(8,128)}) custom-call(s32[3,4,8]{2,1,0:T(4,128)} %bitcast.14, s32[3,2,32]{2,1,0:T(2,128)} %bitcast.16, f32[5,125,128]{2,1,0:T(8,128)} %refs_15_.1, bf16[3,64,128]{2,1,0:T(8,128)(2,1)} %constant.27.clone.refs_3_.refs_6_.refs_7_, bf16[128,320]{1,0:T(8,128)(2,1)} %constant.22.clone.refs_4_), custom_call_target="tpu_custom_call" | custom-call | tf_op jit(solution)/shard_map/pack_kernel/pallas_call | solution.py:671
  3.4 0.0 copy-start.3
  3.4 0.0 copy-start.2
  3.4 13.9 %all-to-all-start = ((f32[8,16,128]{2,1,0:T(8,128)}), f32[8,16,128]{2,1,0:T(8,128)S(1)}, u32[]{:S(2)}, u32[]{:S(2)}) async-start(f32[8,16,128]{2,1,0:T(8,128)} %bitcast.11), calls=%async_computation | async-start | bytes 131072 | tf_op jit(solution)/shard_map/all_to_all | solution.py:694
  17.3 0.0 copy-done.3
  17.3 1.9 %collective-permute-start = (f32[96,128]{1,0:T(8,128)S(1)}, f32[96,128]{1,0:T(8,128)S(1)}, u32[]{:S(2)}, u32[]{:S(2)}) collective-permute-start(f32[96,128]{1,0:T(8,128)S(1)} %copy-done.3), channel_id=1, source_target_pairs={{0,8},{8,16},{16,24},{24,32},{32,40},{40,48},{48,56},{56,64},{64,7... | collective-permute-start | bytes 147464 | tf_op jit(solution)/shard_map/ppermute | solution.py:695
  19.2 0.0 copy-done.2
  19.3 9.2 %collective-permute-start.1 = (f32[96,128]{1,0:T(8,128)S(1)}, f32[96,128]{1,0:T(8,128)S(1)}, u32[]{:S(2)}, u32[]{:S(2)}) collective-permute-start(f32[96,128]{1,0:T(8,128)S(1)} %copy-done.2), channel_id=1, source_target_pairs={{8,0},{16,8},{24,16},{32,24},{40,32},{48,40},{56,48},{64,56},{72,6... | collective-permute-start | bytes 147464 | tf_op jit(solution)/shard_map/ppermute | solution.py:696
  28.5 3.2 %volume_kernel.1 = (f32[5,128,128]{2,1,0:T(8,128)}, f32[12,128,128]{2,1,0:T(8,128)}) custom-call(f32[5,125,128]{2,1,0:T(8,128)} %refs_15_.1, bf16[3,128,256]{2,1,0:T(8,128)(2,1)} %constant.20.clone.refs_1_.refs_6_), custom_call_target="tpu_custom_call" | custom-call | tf_op jit(solution)/shard_map/volume_kernel/pallas_call | solution.py:671
  31.8 0.0 collective-permute-done.refs_1_
  31.8 0.0 collective-permute-done.1.refs_2_
  31.8 0.0 all-to-all-done
  31.8 9.0 %surface_kernel.1 = (f32[5,128,128]{2,1,0:T(8,128)}, f32[3,4,128,128]{3,2,1,0:T(8,128)}, f32[128,128]{1,0:T(8,128)}, f32[96,128]{1,0:T(8,128)}, f32[96,128]{1,0:T(8,128)}) custom-call(f32[128,128]{1,0:T(8,128)S(1)} %bitcast.8, f32[96,128]{1,0:T(8,128)S(1)} %collective-permute-done.refs_1_, f32[96,128]{1,0:T(8,128)S(1)} %collective-permute-done.1.refs_2_, ...), custom_call_target="tpu_custom_call" | custom-call | tf_op jit(solution)/shard_map/surface_kernel/pallas_call | solution.py:671
  40.8 0.0 copy-start.1
  40.8 0.0 copy-start
  40.8 5.2 %all-to-all-start.1 = ((f32[8,16,128]{2,1,0:T(8,128)}), f32[8,16,128]{2,1,0:T(8,128)S(1)}, u32[]{:S(2)}, u32[]{:S(2)}) async-start(f32[8,16,128]{2,1,0:T(8,128)} %bitcast.10), calls=%async_computation.1 | async-start | bytes 131072 | tf_op jit(solution)/shard_map/all_to_all | solution.py:694
  46.1 0.0 copy-done.1
  46.1 1.9 %collective-permute-start.2 = (f32[96,128]{1,0:T(8,128)S(1)}, f32[96,128]{1,0:T(8,128)S(1)}, u32[]{:S(2)}, u32[]{:S(2)}) collective-permute-start(f32[96,128]{1,0:T(8,128)S(1)} %copy-done.1), channel_id=1, source_target_pairs={{0,8},{8,16},{16,24},{24,32},{32,40},{40,48},{48,56},{56,64},{64,7... | collective-permute-start | bytes 147464 | tf_op jit(solution)/shard_map/ppermute | solution.py:695
  48.0 0.0 copy-done
  48.0 6.9 %collective-permute-start.3 = (f32[96,128]{1,0:T(8,128)S(1)}, f32[96,128]{1,0:T(8,128)S(1)}, u32[]{:S(2)}, u32[]{:S(2)}) collective-permute-start(f32[96,128]{1,0:T(8,128)S(1)} %copy-done), channel_id=1, source_target_pairs={{8,0},{16,8},{24,16},{32,24},{40,32},{48,40},{56,48},{64,56},{72,6... | collective-permute-start | bytes 147464 | tf_op jit(solution)/shard_map/ppermute | solution.py:696
  54.9 0.0 collective-permute-done.2.refs_1_
  54.9 1.0 %collective-permute-done.3.refs_2_ = f32[96,128]{1,0:T(8,128)S(1)} collective-permute-done((f32[96,128]{1,0:T(8,128)S(1)}, f32[96,128]{1,0:T(8,128)S(1)}, u32[]{:S(2)}, u32[]{:S(2)}) %collective-permute-start.3) | collective-permute-done | bytes 49184 | tf_op jit(solution)/shard_map/ppermute | solution.py:696
  55.8 0.0 all-to-all-done.1
  55.8 5.9 %final_kernel.1 = (f32[5,125,128]{2,1,0:T(8,128)}, f32[5,125,128]{2,1,0:T(8,128)}) custom-call(f32[128,128]{1,0:T(8,128)S(1)} %bitcast.9, f32[96,128]{1,0:T(8,128)S(1)} %collective-permute-done.2.refs_1_, f32[96,128]{1,0:T(8,128)S(1)} %collective-permute-done.3.refs_2_, s32[6,128]{1,0:T(8,128)} %refs_3_.4, s32[6,4,128]{2,1,0:T(4,128)} %bitcast.13, ...), custom_call_target="tpu_custom_call" | custom-call | tf_op jit(solution)/shard_map/final_kernel/pallas_call | solution.py:671
Async XLA Ops:
  3.4 13.9 %copy-start.3 = (f32[96,128]{1,0:T(8,128)S(1)}, f32[96,128]{1,0:T(8,128)}, u32[]{:S(2)}) copy-start(f32[96,128]{1,0:T(8,128)} %get-tuple-element.13) | copy-start | bytes 147460
  3.4 15.8 %copy-start.2 = (f32[96,128]{1,0:T(8,128)S(1)}, f32[96,128]{1,0:T(8,128)}, u32[]{:S(2)}) copy-start(f32[96,128]{1,0:T(8,128)} %get-tuple-element.14) | copy-start | bytes 147460
  3.4 28.4 %all-to-all-start = ((f32[8,16,128]{2,1,0:T(8,128)}), f32[8,16,128]{2,1,0:T(8,128)S(1)}, u32[]{:S(2)}, u32[]{:S(2)}) async-start(f32[8,16,128]{2,1,0:T(8,128)} %bitcast.11), calls=%async_computation | async-start | bytes 131072 | tf_op jit(solution)/shard_map/all_to_all | solution.py:694
  17.3 14.4 %collective-permute-start = (f32[96,128]{1,0:T(8,128)S(1)}, f32[96,128]{1,0:T(8,128)S(1)}, u32[]{:S(2)}, u32[]{:S(2)}) collective-permute-start(f32[96,128]{1,0:T(8,128)S(1)} %copy-done.3), channel_id=1, source_target_pairs={{0,8},{8,16},{16,24},{24,32},{32,40},{40,48},{48,56},{56,64},{64,7... | collective-permute-start | bytes 147464 | tf_op jit(solution)/shard_map/ppermute | solution.py:695
  19.3 12.5 %collective-permute-start.1 = (f32[96,128]{1,0:T(8,128)S(1)}, f32[96,128]{1,0:T(8,128)S(1)}, u32[]{:S(2)}, u32[]{:S(2)}) collective-permute-start(f32[96,128]{1,0:T(8,128)S(1)} %copy-done.2), channel_id=1, source_target_pairs={{8,0},{16,8},{24,16},{32,24},{40,32},{48,40},{56,48},{64,56},{72,6... | collective-permute-start | bytes 147464 | tf_op jit(solution)/shard_map/ppermute | solution.py:696
  40.8 5.2 %copy-start.1 = (f32[96,128]{1,0:T(8,128)S(1)}, f32[96,128]{1,0:T(8,128)}, u32[]{:S(2)}) copy-start(f32[96,128]{1,0:T(8,128)} %get-tuple-element.18) | copy-start | bytes 147460
  40.8 7.2 %copy-start = (f32[96,128]{1,0:T(8,128)S(1)}, f32[96,128]{1,0:T(8,128)}, u32[]{:S(2)}) copy-start(f32[96,128]{1,0:T(8,128)} %get-tuple-element.19) | copy-start | bytes 147460
  40.8 15.0 %all-to-all-start.1 = ((f32[8,16,128]{2,1,0:T(8,128)}), f32[8,16,128]{2,1,0:T(8,128)S(1)}, u32[]{:S(2)}, u32[]{:S(2)}) async-start(f32[8,16,128]{2,1,0:T(8,128)} %bitcast.10), calls=%async_computation.1 | async-start | bytes 131072 | tf_op jit(solution)/shard_map/all_to_all | solution.py:694
  46.1 8.8 %collective-permute-start.2 = (f32[96,128]{1,0:T(8,128)S(1)}, f32[96,128]{1,0:T(8,128)S(1)}, u32[]{:S(2)}, u32[]{:S(2)}) collective-permute-start(f32[96,128]{1,0:T(8,128)S(1)} %copy-done.1), channel_id=1, source_target_pairs={{0,8},{8,16},{16,24},{24,32},{32,40},{40,48},{48,56},{56,64},{64,7... | collective-permute-start | bytes 147464 | tf_op jit(solution)/shard_map/ppermute | solution.py:695
  48.0 7.8 %collective-permute-start.3 = (f32[96,128]{1,0:T(8,128)S(1)}, f32[96,128]{1,0:T(8,128)S(1)}, u32[]{:S(2)}, u32[]{:S(2)}) collective-permute-start(f32[96,128]{1,0:T(8,128)S(1)} %copy-done), channel_id=1, source_target_pairs={{8,0},{16,8},{24,16},{32,24},{40,32},{48,40},{56,48},{64,56},{72,6... | collective-permute-start | bytes 147464 | tf_op jit(solution)/shard_map/ppermute | solution.py:696
